TPU v7x, 32 devices: a whole 2x2x4 slice. The times are simulated.
32 devices in a mesh: de: 8 (over z, x), tp: 4 (over y, core).
Axes of the slice: x: 2, y: 2, z: 4, core: 2. Of those that a mesh axis runs over, the one named last changes fastest.
Arguments:
- raw_tiles: bfloat16 [4, 128, 512], P(None, ('de', 'tp')), may hold values from -6 to 6
- stem_weight: bfloat16 [48, 4, 3, 3], replicated, may hold values from -1 to 1
- embed_weight: bfloat16 [768, 1024], replicated, may hold values from -0.21875 to 0.21875
- norm_gain: float32 [1024], replicated, may hold values from 0.1 to 1.9
- router_weight: bfloat16 [1024, 8], replicated, may hold values from -0.1875 to 0.1875
- w_gate: bfloat16 [8, 1024, 4096], P('de', None, 'tp'), may hold values from -0.1875 to 0.1875
- w_up: bfloat16 [8, 1024, 4096], P('de', None, 'tp'), may hold values from -0.1875 to 0.1875
- w_down: bfloat16 [8, 4096, 1024], P('de', 'tp'), may hold values from -0.09375 to 0.09375
- routes: int32 [4096, 1], P(('de', 'tp')), may hold values from 0 to 7; in each aligned block of 128 rows (0 to 127, 128 to 255, ...) at most 32 rows name the same one
- cotangent: bfloat16 [4096, 1024], P(('de', 'tp')), may hold values from -6 to 6
Outputs:
- expert_mix: bfloat16 [4096, 1024], P(('de', 'tp'))
- grad_gate: float32 [8, 1024, 4096], P('de', None, 'tp')
- grad_up: float32 [8, 1024, 4096], P('de', None, 'tp')
- grad_down: float32 [8, 4096, 1024], P('de', 'tp')
- grad_router: float32 [1024, 8], replicated
- grad_gain: float32 [1024], replicated
- grad_embed: float32 [768, 1024], replicated
- grad_stem: float32 [48, 4, 3, 3], replicated
Inputs may be any that keep to these rules, and one draw needn't show every extreme that they name: `routes`: within the tokens of one tile no expert is named more than 32 times, and in every draw some expert is named exactly 32 times in some tile.
All inputs are finite; a program needn't handle non-finite values.
Results may differ from a plain program's by a relative error of at most 0.0092.
Values may be sent and summed in bfloat16 or wider, within the bound.
A program may use at most 128 MiB of HBM per device.

v0:
```python
import jax
import jax.numpy as jnp
from jax import lax
from jax.sharding import PartitionSpec as P

PATCH = 4


GELU_C = 0.7978845608028654
GELU_A = 0.044715
EPSILON = 1e-06


def padded_2(block, sides, width):
    for axis, dim in sides:
        count = lax.axis_size(axis)
        forward = [(i, i + 1) for i in range(count - 1)]
        backward = [(target, source) for source, target in forward]
        low = lax.ppermute(
            lax.slice_in_dim(block, block.shape[dim] - width, None, axis=dim), axis, forward
        )
        high = lax.ppermute(lax.slice_in_dim(block, 0, width, axis=dim), axis, backward)
        block = jnp.concatenate([low, block, high], axis=dim)
    return block


def gelu_value(preact):
    tanh_v = jnp.tanh(GELU_C * (preact + GELU_A * preact * preact * preact))
    return 0.5 * preact * (1.0 + tanh_v)


def gelu_slope(preact):
    tanh_v = jnp.tanh(GELU_C * (preact + GELU_A * preact * preact * preact))
    return 0.5 * (1.0 + tanh_v) + 0.5 * preact * (1.0 - tanh_v * tanh_v) * GELU_C * (
        1.0 + 3.0 * GELU_A * preact * preact
    )


def stem_stack(padded):
    pixel_rows = padded.shape[1] - 2
    pixel_cols = padded.shape[2]
    widened = jnp.pad(padded, ((0, 0), (0, 0), (1, 1)))
    pieces = [
        widened[:, row_step : row_step + pixel_rows, col_step : col_step + pixel_cols]
        for row_step in range(3)
        for col_step in range(3)
    ]
    stacked = jnp.stack(pieces, axis=1)
    return stacked.reshape(36, pixel_rows * pixel_cols)


def patchify(feature_b, pixel_rows, pixel_cols):
    channels = feature_b.shape[0]
    patch_grid = feature_b.reshape(channels, pixel_rows // PATCH, PATCH, pixel_cols // PATCH, PATCH)
    patch_grid = patch_grid.transpose(1, 3, 0, 2, 4)
    return patch_grid.reshape(pixel_rows // PATCH * (pixel_cols // PATCH), channels * PATCH * PATCH)


def unpatchify(patch_cot, pixel_rows, pixel_cols, channels):
    patch_grid = patch_cot.reshape(pixel_rows // PATCH, pixel_cols // PATCH, channels, PATCH, PATCH)
    patch_grid = patch_grid.transpose(2, 0, 3, 1, 4)
    return patch_grid.reshape(channels, pixel_rows * pixel_cols)


def front(padded, stem_weight, embed_weight, norm_gain):
    pixel_rows = padded.shape[1] - 2
    pixel_cols = padded.shape[2]
    stacked = stem_stack(padded)
    kernel = stem_weight.reshape(stem_weight.shape[0], 36)
    preact = jnp.dot(kernel, stacked, preferred_element_type=jnp.float32)
    feature_b = gelu_value(preact).astype(jnp.bfloat16)
    patches_b = patchify(feature_b, pixel_rows, pixel_cols)
    embedded = jnp.dot(patches_b, embed_weight, preferred_element_type=jnp.float32)
    inv_rms = lax.rsqrt(jnp.mean(embedded * embedded, axis=-1, keepdims=True) + EPSILON)
    hidden_b = (embedded * inv_rms * norm_gain).astype(jnp.bfloat16)
    return (stacked, preact, patches_b, embedded, inv_rms, hidden_b)


def back_front(
    stacked,
    preact,
    patches_b,
    embedded,
    inv_rms,
    norm_gain,
    embed_weight,
    upstream,
    pixel_rows,
    pixel_cols,
):
    normed = embedded * inv_rms
    scaled = upstream * norm_gain
    embed_in = inv_rms * (scaled - normed * jnp.mean(scaled * normed, axis=-1, keepdims=True))
    gain_part = jnp.sum(upstream * normed, axis=0)
    embed_cot = embed_in.astype(jnp.bfloat16)
    embed_part = jnp.dot(patches_b.T, embed_cot, preferred_element_type=jnp.float32)
    patch_cot = jnp.dot(embed_cot, embed_weight.T, preferred_element_type=jnp.float32)
    feature_cot = unpatchify(patch_cot, pixel_rows, pixel_cols, preact.shape[0])
    preact_cot = (feature_cot * gelu_slope(preact)).astype(jnp.bfloat16)
    stem_part = jnp.dot(preact_cot, stacked.T, preferred_element_type=jnp.float32)
    return (gain_part, embed_part, stem_part)


def slot_index(route_rows, experts, capacity):
    chosen = route_rows.reshape(-1)
    onehot = (chosen[:, None] == jnp.arange(experts, dtype=jnp.int32)[None, :]).astype(jnp.int32)
    before = jnp.cumsum(onehot, axis=0) - onehot
    slot_pos = jnp.sum(before * onehot, axis=1)
    return chosen * capacity + slot_pos


def gate_scores(logits, routes):
    picked = jnp.take_along_axis(logits, routes, axis=1)
    return jax.nn.sigmoid(picked)


def router_cot(score_grad, gate_score, routes, experts):
    local_grad = score_grad * gate_score * (1.0 - gate_score)
    chosen_hot = (routes[:, :, None] == jnp.arange(experts, dtype=jnp.int32)[None, None, :]).astype(
        jnp.float32
    )
    return jnp.sum(chosen_hot * local_grad[:, :, None], axis=1).astype(jnp.bfloat16)


def dispatch(buffer):
    moved = lax.all_to_all(buffer, "de", split_axis=0, concat_axis=0, tiled=True)
    return lax.all_gather(moved[None], "tp", axis=0, tiled=True)


def collect(partial_term, total_rows, experts, capacity, model_width):
    members = lax.axis_size("tp")
    own_share = lax.psum_scatter(
        partial_term(jnp.int32(0), total_rows // members * lax.axis_size("tp")),
        "tp",
        scatter_dimension=0,
        tiled=True,
    )
    share_b = own_share.astype(jnp.bfloat16).reshape(experts, capacity, model_width)
    returned = lax.all_to_all(share_b, "de", split_axis=0, concat_axis=0, tiled=True)
    return returned.reshape(experts * capacity, model_width)


def local(
    raw_tiles,
    stem_weight,
    embed_weight,
    norm_gain,
    router_weight,
    w_gate,
    w_up,
    w_down,
    routes,
    cotangent,
):
    tok_dev = cotangent.shape[0]
    model_width = cotangent.shape[1]
    top_count = routes.shape[1]
    local_experts = w_gate.shape[0]
    hidden_share = w_gate.shape[2]
    owners = lax.axis_size("de")
    members = lax.axis_size("tp")
    experts = local_experts * owners
    capacity = 2 * tok_dev * top_count // experts
    pixel_rows = raw_tiles.shape[1]
    pixel_cols = raw_tiles.shape[2]
    padded = padded_2(raw_tiles, ((("de", "tp"), 1),), 1)
    stacked, preact, patches_b, embedded, inv_rms, hidden_b = front(
        padded, stem_weight, embed_weight, norm_gain
    )
    logits = jnp.dot(hidden_b, router_weight, preferred_element_type=jnp.float32)
    gate_score = gate_scores(logits, routes)
    slot_flat = slot_index(routes, experts, capacity)
    selector = (
        slot_flat[None, :] == jnp.arange(experts * capacity, dtype=jnp.int32)[:, None]
    ).astype(jnp.bfloat16)
    hidden_pairs = jnp.repeat(hidden_b, top_count, axis=0)
    cot_pairs = jnp.repeat(cotangent.astype(jnp.float32), top_count, axis=0)
    out_cot = (gate_score * cot_pairs).astype(jnp.bfloat16)
    sent_rows = jnp.dot(selector, hidden_pairs, preferred_element_type=jnp.float32).astype(
        jnp.bfloat16
    )
    sent_cots = jnp.dot(selector, out_cot, preferred_element_type=jnp.float32).astype(jnp.bfloat16)
    group_shape = (members, owners, local_experts, capacity, model_width)
    group_rows = dispatch(sent_rows.reshape(experts, capacity, model_width)).reshape(group_shape)
    group_cots = dispatch(sent_cots.reshape(experts, capacity, model_width)).reshape(group_shape)
    gate_proj = jnp.einsum(
        "tslcx,lxf->tslcf", group_rows, w_gate, preferred_element_type=jnp.float32
    )
    up_proj = jnp.einsum("tslcx,lxf->tslcf", group_rows, w_up, preferred_element_type=jnp.float32)
    sigmoid_gate = jax.nn.sigmoid(gate_proj)
    activated = gate_proj * sigmoid_gate
    hidden_act = (activated * up_proj).astype(jnp.bfloat16)
    total_rows = members * owners * local_experts * capacity
    slot_block = local_experts * capacity

    def forward_term(first_row, row_count):
        rows_part = hidden_act.reshape(total_rows, hidden_share)
        rows_part = rows_part.reshape(
            row_count // slot_block, local_experts, capacity, hidden_share
        )
        product = jnp.einsum(
            "blcf,lfx->blcx", rows_part, w_down, preferred_element_type=jnp.float32
        )
        return product.reshape(row_count, model_width)

    out_flat = collect(forward_term, total_rows, experts, capacity, model_width)
    out_wide = jnp.take(out_flat, slot_flat, axis=0).astype(jnp.float32)
    expert_mix = jnp.sum(
        (gate_score * out_wide).reshape(tok_dev, top_count, model_width), axis=1
    ).astype(jnp.bfloat16)
    score_grad = jnp.sum(cot_pairs * out_wide, axis=-1).reshape(tok_dev, top_count)
    logit_cot = router_cot(score_grad, gate_score, routes, experts)
    router_part = jnp.dot(hidden_b.T, logit_cot, preferred_element_type=jnp.float32)
    router_total = lax.psum(router_part, ("de", "tp"))
    act_cot = jnp.einsum("tslcx,lfx->tslcf", group_cots, w_down, preferred_element_type=jnp.float32)
    gate_cot = (
        act_cot * up_proj * (sigmoid_gate * (1.0 + gate_proj * (1.0 - sigmoid_gate)))
    ).astype(jnp.bfloat16)
    up_cot = (act_cot * activated).astype(jnp.bfloat16)
    grad_gate = jnp.einsum(
        "tslcx,tslcf->lxf", group_rows, gate_cot, preferred_element_type=jnp.float32
    )
    grad_up = jnp.einsum("tslcx,tslcf->lxf", group_rows, up_cot, preferred_element_type=jnp.float32)
    grad_down = jnp.einsum(
        "tslcf,tslcx->lfx", hidden_act, group_cots, preferred_element_type=jnp.float32
    )

    def backward_term(first_row, row_count):
        gate_part = gate_cot.reshape(total_rows, hidden_share)
        up_part = up_cot.reshape(total_rows, hidden_share)
        gate_part = gate_part.reshape(
            row_count // slot_block, local_experts, capacity, hidden_share
        )
        up_part = up_part.reshape(row_count // slot_block, local_experts, capacity, hidden_share)
        product = jnp.einsum(
            "blcf,lxf->blcx", gate_part, w_gate, preferred_element_type=jnp.float32
        )
        product = product + jnp.einsum(
            "blcf,lxf->blcx", up_part, w_up, preferred_element_type=jnp.float32
        )
        return product.reshape(row_count, model_width)

    cot_flat = collect(backward_term, total_rows, experts, capacity, model_width)
    cot_back = jnp.take(cot_flat, slot_flat, axis=0).astype(jnp.float32)
    upstream = jnp.sum(cot_back.reshape(tok_dev, top_count, model_width), axis=1)
    upstream = upstream + jnp.dot(logit_cot, router_weight.T, preferred_element_type=jnp.float32)
    gain_part, embed_part, stem_part = back_front(
        stacked,
        preact,
        patches_b,
        embedded,
        inv_rms,
        norm_gain,
        embed_weight,
        upstream,
        pixel_rows,
        pixel_cols,
    )
    gain_total, embed_total, stem_total = lax.psum((gain_part, embed_part, stem_part), ("de", "tp"))
    return (
        expert_mix,
        grad_gate,
        grad_up,
        grad_down,
        router_total,
        gain_total,
        embed_total,
        stem_total.reshape(stem_weight.shape),
    )


def solution(mesh):
    return jax.shard_map(
        local,
        mesh=mesh,
        in_specs=(
            P(None, ("de", "tp"), None),
            P(),
            P(),
            P(),
            P(),
            P("de", None, "tp"),
            P("de", None, "tp"),
            P("de", "tp", None),
            P(("de", "tp"), None),
            P(("de", "tp"), None),
        ),
        out_specs=(
            P(("de", "tp"), None),
            P("de", None, "tp"),
            P("de", None, "tp"),
            P("de", "tp", None),
            P(),
            P(),
            P(),
            P(),
        ),
        check_vma=False,
    )
```

profile of v0, /device:TPU:0, one launch (start us, length us, event | category | flops | bytes accessed | tf_op | source)
XLA Modules:
  0.0 423.3 jit_solution(13596884655805119971)
XLA Ops:
  8.1 2.4 collective-permute-start
  10.5 1.3 collective-permute-start.1
  19.3 1.0 multiply_convert_fusion.2
  20.9 2.0 multiply_reduce_fusion.2
  23.3 22.9 %all_to_all.20 = bf16[8,32,1024]{2,1,0:T(8,128)(2,1)} all-to-all(bf16[8,32,1024]{2,1,0:T(8,128)(2,1)S(1)} %bitcast.244), channel_id=1, replica_groups=mesh['de'=8,'tp'=4] {'de'}, dimensions={0} | all-to-all | bytes 1048576 | tf_op jit(solution)/shard_map/all_to_all | solution.py:126
  46.3 22.4 %all-gather.5.cloned.1.call-done = bf16[32,32,1024]{2,1,0:T(8,128)(2,1)} async-done(((bf16[8,32,1024]{2,1,0:T(8,128)(2,1)}), bf16[32,32,1024]{2,1,0:T(8,128)(2,1)}) %all-gather.5.cloned.1.call-update) | async-done | bytes 2097168 | tf_op jit(solution)/shard_map/all_gather | solution.py:127
  68.7 4.7 %fusion.13 = f32[4,8,32,1024]{3,2,1,0:T(8,128)S(1)} fusion(bf16[4,8,32,1024]{3,2,1,0:T(8,128)(2,1)} %bitcast.258, bf16[1,1024,1024]{2,1,0:T(8,128)(2,1)} %param.17), kind=kOutput, calls=%fused_computation.26 | convolution fusion | flops 2147483648 | bytes 8388608 | tf_op jit(solution)/shard_map/tslcx,lxf->tslcf/dot_general | solution.py:186
  73.4 4.7 %fusion.3 = (bf16[4,8,1,32,1024]{4,3,1,0,2:T(8,128)(2,1)S(1)}, f32[4,8,32,1024]{3,2,1,0:T(8,128)}) fusion(f32[4,8,32,1024]{3,2,1,0:T(8,128)S(1)} %fusion.13, bf16[4,8,32,1024]{3,2,1,0:T(8,128)(2,1)S(1)} %bitcast.261, bf16[1,1024,1024]{2,1,0:T(8,128)(2,1)S(1)} %copy-done.12), kind=kOutput, calls=%fused_computation.9 | convolution fusion | flops 2153775104 | bytes 14680064 | tf_op jit(solution)/shard_map/tslcx,lxf->tslcf/dot_general | solution.py:189
  78.1 4.4 %fusion.19 = f32[32,32,1024]{2,1,0:T(8,128)} fusion(bf16[32,32,1024]{2,1,0:T(8,128)(2,1)S(1)} %bitcast.264, bf16[1,1024,1024]{2,1,0:T(8,128)(2,1)S(1)} %copy-done), kind=kOutput, calls=%fused_computation.32 | convolution fusion | flops 2147483648 | bytes 8388608 | tf_op jit(solution)/shard_map/blcf,lfx->blcx/dot_general | solution.py:201
  82.5 44.6 %reduce-scatter.3.cloned.1.call-done = f32[256,1024]{1,0:T(8,128)} async-done(((f32[1024,1024]{1,0:T(8,128)}), f32[256,1024]{1,0:T(8,128)}) %reduce-scatter.3.cloned.1.call-update) | async-done | bytes 1048592 | tf_op jit(solution)/shard_map/reduce_scatter | solution.py:132
  127.2 2.1 convert_element_type.63
  129.3 5.5 %all-to-all-start.1 = ((bf16[8,32,1024]{2,1,0:T(8,128)(2,1)}), bf16[8,32,1024]{2,1,0:T(8,128)(2,1)S(1)}, u32[]{:S(2)}, u32[]{:S(2)}) async-start(bf16[8,32,1024]{2,1,0:T(8,128)(2,1)} %bitcast.241), calls=%async_computation.2 | async-start | bytes 1048576 | tf_op jit(solution)/shard_map/all_to_all | solution.py:139
  135.1 1.0 gather_fusion
  136.1 13.1 %all-to-all-done.1 = bf16[8,32,1024]{2,1,0:T(8,128)(2,1)S(1)} async-done(((bf16[8,32,1024]{2,1,0:T(8,128)(2,1)}), bf16[8,32,1024]{2,1,0:T(8,128)(2,1)S(1)}, u32[]{:S(2)}, u32[]{:S(2)}) %all-to-all-start.1) | async-done | bytes 524320 | tf_op jit(solution)/shard_map/all_to_all | solution.py:139
  150.1 1.2 fusion.32
  151.3 1.3 convolution_convert_fusion
  152.7 18.2 %all_to_all.21 = bf16[8,32,1024]{2,1,0:T(8,128)(2,1)} all-to-all(bf16[8,32,1024]{2,1,0:T(8,128)(2,1)S(1)} %bitcast.243), channel_id=1, replica_groups=mesh['de'=8,'tp'=4] {'de'}, dimensions={0} | all-to-all | bytes 1048576 | tf_op jit(solution)/shard_map/all_to_all | solution.py:126
  171.1 20.6 %all-gather.7.cloned.1.call-done = bf16[32,32,1024]{2,1,0:T(8,128)(2,1)} async-done(((bf16[8,32,1024]{2,1,0:T(8,128)(2,1)}), bf16[32,32,1024]{2,1,0:T(8,128)(2,1)}) %all-gather.7.cloned.1.call-update) | async-done | bytes 2097168 | tf_op jit(solution)/shard_map/all_gather | solution.py:127
  191.8 6.9 %fusion.2 = (bf16[4,8,1,32,1024]{4,3,1,0,2:T(8,128)(2,1)S(1)}, bf16[4,8,1,32,1024]{4,3,1,0,2:T(8,128)(2,1)S(1)}) fusion(f32[4,8,32,1024]{3,2,1,0:T(8,128)} %copy-done.20, f32[4,8,32,1024]{3,2,1,0:T(8,128)} %get-tuple-element.43, bf16[4,8,32,1024]{3,2,1,0:T(8,128)(2,1)} %bitcast.262, bf16[1,1024,1024]{2,1,0:T(8,128)(2,1)S(1)} %copy-done), kind=kOutput, calls=%fused_computation.7 | convolution fusion | flops 2161115136 | bytes 16777216 | tf_op jit(solution)/shard_map/tslcx,lfx->tslcf/dot_general | solution.py:215
  198.8 2.4 fusion.15
  201.8 4.5 %fusion.25 = f32[32,32,1024]{2,1,0:T(8,128)} fusion(f32[32,32,1024]{2,1,0:T(8,128)S(1)} %fusion.15, bf16[32,32,1024]{2,1,0:T(8,128)(2,1)S(1)} %bitcast.265, bf16[1,1024,1024]{2,1,0:T(8,128)(2,1)S(1)} %copy-done.14), kind=kOutput, calls=%fused_computation.38 | convolution fusion | flops 2148532224 | bytes 12582912 | tf_op jit(solution)/shard_map/blcf,lxf->blcx/dot_general | solution.py:235
  208.4 7.0 %convolution_bitcast_fusion.1 = f32[1,1024,1024]{2,1,0:T(8,128)} fusion(bf16[4,8,32,1024]{3,2,1,0:T(8,128)(2,1)} %bitcast.263, bf16[4,8,1,32,1024]{4,3,1,0,2:T(8,128)(2,1)} %copy-done.16), kind=kOutput, calls=%fused_computation.19 | convolution fusion | flops 2147483648 | bytes 8388608 | tf_op jit(solution)/shard_map/tslcf,tslcx->lfx/dot_general | solution.py:224
  215.4 35.6 %reduce-scatter.5.cloned.1.call-done = f32[256,1024]{1,0:T(8,128)} async-done(((f32[1024,1024]{1,0:T(8,128)}), f32[256,1024]{1,0:T(8,128)}) %reduce-scatter.5.cloned.1.call-update) | async-done | bytes 1048592 | tf_op jit(solution)/shard_map/reduce_scatter | solution.py:132
  251.0 2.1 convert_element_type.72
  253.1 5.5 %all-to-all-start.3 = ((bf16[8,32,1024]{2,1,0:T(8,128)(2,1)}), bf16[8,32,1024]{2,1,0:T(8,128)(2,1)S(1)}, u32[]{:S(2)}, u32[]{:S(2)}) async-start(bf16[8,32,1024]{2,1,0:T(8,128)(2,1)} %bitcast.77), calls=%async_computation.5 | async-start | bytes 1048576 | tf_op jit(solution)/shard_map/all_to_all | solution.py:139
  258.8 6.6 %convolution_bitcast_fusion.2 = f32[1,1024,1024]{2,1,0:T(8,128)} fusion(bf16[4,8,32,1024]{3,2,1,0:T(8,128)(2,1)} %bitcast.259, bf16[4,8,1,32,1024]{4,3,1,0,2:T(8,128)(2,1)} %copy-done.18), kind=kOutput, calls=%fused_computation.20 | convolution fusion | flops 2147483648 | bytes 8388608 | tf_op jit(solution)/shard_map/tslcx,tslcf->lxf/dot_general | solution.py:223
  265.5 7.6 %all-to-all-done.3 = bf16[8,32,1024]{2,1,0:T(8,128)(2,1)S(1)} async-done(((bf16[8,32,1024]{2,1,0:T(8,128)(2,1)}), bf16[8,32,1024]{2,1,0:T(8,128)(2,1)S(1)}, u32[]{:S(2)}, u32[]{:S(2)}) %all-to-all-start.3) | async-done | bytes 524320 | tf_op jit(solution)/shard_map/all_to_all | solution.py:139
  274.6 2.2 fusion.74
  276.8 6.7 %convolution_bitcast_fusion.3 = f32[1,1024,1024]{2,1,0:T(8,128)} fusion(bf16[4,8,32,1024]{3,2,1,0:T(8,128)(2,1)} %bitcast.260, bf16[4,8,1,32,1024]{4,3,1,0,2:T(8,128)(2,1)} %copy-done.17), kind=kOutput, calls=%fused_computation.21 | convolution fusion | flops 2147483648 | bytes 8388608 | tf_op jit(solution)/shard_map/tslcx,tslcf->lxf/dot_general | solution.py:220
  285.3 40.0 %all-reduce.1 = (f32[1024,8]{0,1:T(8,128)}, f32[1024]{0:T(1024)}, f32[48,4,3,3]{0,3,2,1:T(4,128)S(1)}) all-reduce(f32[1024,8]{0,1:T(8,128)S(1)} %fusion.51, f32[1024]{0:T(1024)S(1)} %get-tuple-element.26, f32[48,4,3,3]{0,3,2,1:T(4,128)S(1)} %reshape.230), channel_id=1, replica_groups=mesh['de'=8,'tp'=4] {'de','tp'}, use_global_device_ids=true, to_apply=%region_5.7 | all-reduce | flops 10944 | bytes 87552 | tf_op jit(solution)/shard_map/psum | solution.py:214
  325.9 86.7 %all-reduce.4.cloned.1.call-done = f32[768,1024]{1,0:T(8,128)} async-done(((f32[768,1024]{1,0:T(8,128)}), f32[768,1024]{1,0:T(8,128)}) %all-reduce.4.cloned.1.call-update) | async-done | bytes 3145744 | tf_op jit(solution)/shard_map/psum | solution.py:259
  412.7 4.1 copy.83
  (100 shorter events, 17.6 us)
Async XLA Ops:
  7.2 71.0 %copy-start = (bf16[1,1024,1024]{2,1,0:T(8,128)(2,1)S(1)}, bf16[1,1024,1024]{2,1,0:T(8,128)(2,1)}, u32[]{:S(2)}) copy-start(bf16[1,1024,1024]{2,1,0:T(8,128)(2,1)} %param.19) | copy-start | bytes 6291460
  7.2 61.5 %all-gather.5.cloned.1.call-start = ((), (), s32[]{:S(2)}) async-start(), calls=%async_computation.9 | async-start | bytes 2621440 | tf_op jit(solution)/shard_map/all_gather | solution.py:127
  8.1 6.8 %collective-permute-start = (bf16[4,1,512]{2,1,0:T(2,128)(2,1)S(1)}, bf16[4,1,512]{2,1,0:T(2,128)(2,1)S(1)}, u32[]{:S(2)}, u32[]{:S(2)}) collective-permute-start(bf16[4,1,512]{2,1,0:T(2,128)(2,1)S(1)} %get-tuple-element.36), channel_id=1, source_target_pairs={{0,1},{1,2},{2,3},{3,4},{4,5},{5,6},{6,7},{7,8},{8,9},{9,10},{10,1... | collective-permute-start | bytes 12296 | tf_op jit(solution)/shard_map/ppermute | solution.py:19
  10.5 5.2 %collective-permute-start.1 = (bf16[4,1,512]{2,1,0:T(2,128)(2,1)S(1)}, bf16[4,1,512]{2,1,0:T(2,128)(2,1)S(1)}, u32[]{:S(2)}, u32[]{:S(2)}) collective-permute-start(bf16[4,1,512]{2,1,0:T(2,128)(2,1)S(1)} %get-tuple-element.37), channel_id=1, source_target_pairs={{1,0},{2,1},{3,2},{4,3},{5,4},{6,5},{7,6},{8,7},{9,8},{10,9},{11,1... | collective-permute-start | bytes 12296 | tf_op jit(solution)/shard_map/ppermute | solution.py:22
  19.3 1.0 copy-start.7
  20.3 2.6 copy-start.9
  20.9 2.0 copy-start.5
  23.0 111.9 %copy-start.3 = (bf16[128,1024]{1,0:T(8,128)(2,1)}, bf16[128,1024]{1,0:T(8,128)(2,1)S(1)}, u32[]{:S(2)}) copy-start(bf16[128,1024]{1,0:T(8,128)(2,1)S(1)} %multiply_convert_fusion.1) | copy-start | bytes 786436
  46.2 80.9 %reduce-scatter.3.cloned.1.call-start = ((), (), s32[]{:S(2)}) async-start(), calls=%async_computation.6 | async-start | bytes 5242880 | tf_op jit(solution)/shard_map/reduce_scatter | solution.py:132
  68.7 4.7 %copy-start.12 = (bf16[1,1024,1024]{2,1,0:T(8,128)(2,1)S(1)}, bf16[1,1024,1024]{2,1,0:T(8,128)(2,1)}, u32[]{:S(2)}) copy-start(bf16[1,1024,1024]{2,1,0:T(8,128)(2,1)} %param.18) | copy-start | bytes 6291460
  68.7 4.7 %copy-start.15 = (bf16[32,32,1024]{2,1,0:T(8,128)(2,1)S(1)}, bf16[32,32,1024]{2,1,0:T(8,128)(2,1)}, u32[]{:S(2)}) copy-start(bf16[32,32,1024]{2,1,0:T(8,128)(2,1)} %all-gather.5.cloned.1.call-done) | copy-start | bytes 6291460
  73.4 4.7 %copy-start.20 = (f32[4,8,32,1024]{3,2,1,0:T(8,128)}, f32[4,8,32,1024]{3,2,1,0:T(8,128)S(1)}, u32[]{:S(2)}) copy-start(f32[4,8,32,1024]{3,2,1,0:T(8,128)S(1)} %fusion.13) | copy-start | bytes 12582916
  78.1 4.4 %copy-start.16 = (bf16[4,8,1,32,1024]{4,3,1,0,2:T(8,128)(2,1)}, bf16[4,8,1,32,1024]{4,3,1,0,2:T(8,128)(2,1)S(1)}, u32[]{:S(2)}) copy-start(bf16[4,8,1,32,1024]{4,3,1,0,2:T(8,128)(2,1)S(1)} %get-tuple-element.42) | copy-start | bytes 6291460
  82.5 52.3 %copy-start.11 = (s32[128,1]{0,1:T(1,128)S(1)}, s32[128,1]{0,1:T(1,128)}, u32[]{:S(2)}) copy-start(s32[128,1]{0,1:T(1,128)} %param.20) | copy-start | bytes 1540
  82.5 52.4 %copy-start.10 = (bf16[1024,8]{0,1:T(8,128)(2,1)S(1)}, bf16[1024,8]{0,1:T(8,128)(2,1)}, u32[]{:S(2)}) copy-start(bf16[1024,8]{0,1:T(8,128)(2,1)} %param.16) | copy-start | bytes 49156
  129.3 20.0 %all-to-all-start.1 = ((bf16[8,32,1024]{2,1,0:T(8,128)(2,1)}), bf16[8,32,1024]{2,1,0:T(8,128)(2,1)S(1)}, u32[]{:S(2)}, u32[]{:S(2)}) async-start(bf16[8,32,1024]{2,1,0:T(8,128)(2,1)} %bitcast.241), calls=%async_computation.2 | async-start | bytes 1048576 | tf_op jit(solution)/shard_map/all_to_all | solution.py:139
  134.8 57.0 %all-gather.7.cloned.1.call-start = ((), (), s32[]{:S(2)}) async-start(), calls=%async_computation.10 | async-start | bytes 2621440 | tf_op jit(solution)/shard_map/all_gather | solution.py:127
  170.9 80.1 %reduce-scatter.5.cloned.1.call-start = ((), (), s32[]{:S(2)}) async-start(), calls=%async_computation.7 | async-start | bytes 5242880 | tf_op jit(solution)/shard_map/reduce_scatter | solution.py:132
  191.8 7.0 %copy-start.13 = (bf16[1,1024,1024]{2,1,0:T(8,128)(2,1)S(1)}, bf16[1,1024,1024]{2,1,0:T(8,128)(2,1)}, u32[]{:S(2)}) copy-start(bf16[1,1024,1024]{2,1,0:T(8,128)(2,1)} %param.18) | copy-start | bytes 6291460
  198.7 2.4 copy-start.18
  198.7 2.4 copy-start.17
  198.7 3.1 copy-start.14
  206.3 0.9 copy-start.4
  253.1 20.0 %all-to-all-start.3 = ((bf16[8,32,1024]{2,1,0:T(8,128)(2,1)}), bf16[8,32,1024]{2,1,0:T(8,128)(2,1)S(1)}, u32[]{:S(2)}, u32[]{:S(2)}) async-start(bf16[8,32,1024]{2,1,0:T(8,128)(2,1)} %bitcast.77), calls=%async_computation.5 | async-start | bytes 1048576 | tf_op jit(solution)/shard_map/all_to_all | solution.py:139
  258.6 154.1 %all-reduce.4.cloned.1.call-start = ((), (), s32[]{:S(2)}) async-start(), calls=%async_computation.8 | async-start | bytes 6291456 | tf_op jit(solution)/shard_map/psum | solution.py:259
  273.1 1.5 copy-start.6
  276.8 6.8 %copy-start.2 = (bf16[768,1024]{1,0:T(8,128)(2,1)S(1)}, bf16[768,1024]{1,0:T(8,128)(2,1)}, u32[]{:S(2)}) copy-start(bf16[768,1024]{1,0:T(8,128)(2,1)} %param.14) | copy-start | bytes 4718596
  283.6 1.3 copy-start.8
  283.6 1.3 copy-start.19
  412.7 4.1 copy-start.1
Sparse Core Ops, SparseCore 0:
  46.4 22.2 all-gather.4
  82.6 44.4 reduce-scatter.2
  171.0 20.7 all-gather.6
  206.5 44.4 reduce-scatter.4
  276.9 135.7 all-reduce.3
where the time goes:
time: 424 us; the launch traced here: 423 us
  waiting for transfers between devices  232 us (55%)
  blocking collectives  81.1 us (19%)
  matrix products  56.5 us (13%)
  starting transfers between devices  15.3 us (4%)
  between operations  14.2 us (3%)
  local copies, waits for them, and re-layouts  13.3 us (3%)
  other arithmetic  11.3 us (3%)
    psum x1, waiting for transfers between devices, local(): lax.psum((gain_part, embed_part, stem_part), ('de', 'tp'))  86.7 us
    reduce_scatter x2, waiting for transfers between devices, collect(): lax.psum_scatter(partial_term(jnp.int32(0), total_rows // members * lax.a...  80.2 us
    all_gather x2, waiting for transfers between devices, dispatch(): return lax.all_gather(moved[None], 'tp', axis=0, tiled=True)  43.1 us
    all_to_all x2, blocking collectives, dispatch(): lax.all_to_all(buffer, 'de', split_axis=0, concat_axis=0, tiled=True)  41.1 us
    psum x1, blocking collectives, local(): router_total = lax.psum(router_part, ('de', 'tp'))  40 us
    all_to_all x2, waiting for transfers between devices, collect(): lax.all_to_all(share_b, 'de', split_axis=0, concat_axis=0, tiled=True)  20.8 us
    all_to_all x2, starting transfers between devices, collect(): lax.all_to_all(share_b, 'de', split_axis=0, concat_axis=0, tiled=True)  11 us
  transfers between devices with their start and end apart: 9, of which 8 were waited for; matrix products, arithmetic and copies ran while one was open for 7% of the time, Pallas kernels for 0%

commit v1 on v0

v1 whole, which is shorter than its diff:
```python
import functools

import jax
import jax.numpy as jnp
import numpy as np
from jax import lax
from jax.experimental import pallas as pl
from jax.experimental.pallas import tpu as pltpu
from jax.sharding import PartitionSpec as P

PATCH = 4
GELU_C = 0.7978845608028654
GELU_A = 0.044715
EPSILON = 1e-06
TAPS = 40
CLASSES = PATCH * PATCH
MESH = pl.DeviceIdType.MESH
BF = jnp.bfloat16
F32 = jnp.float32
VMEM = pl.BlockSpec(memory_space=pltpu.VMEM)
NT = (((1,), (1,)), ((), ()))
TN = (((0,), (0,)), ((), ()))


def mm(a, b, dims=(((1,), (0,)), ((), ())), precision=None):
    return lax.dot_general(a, b, dims, preferred_element_type=F32, precision=precision)


def tap_table(channels):
    side = PATCH + 2
    table = np.zeros((channels * side * side, CLASSES * TAPS), np.float32)
    for q in range(CLASSES):
        for i in range(channels):
            for a in range(3):
                for b in range(3):
                    row = (i * side + q // PATCH + a) * side + q % PATCH + b
                    table[row, q * TAPS + i * 9 + a * 3 + b] = 1.0
    return table


def windows(raw):
    axes = ("de", "tp")
    count = lax.axis_size(axes)
    forward = [(i, i + 1) for i in range(count - 1)]
    backward = [(b, a) for a, b in forward]
    low = lax.ppermute(raw[:, -1:], axes, forward)
    high = lax.ppermute(raw[:, :1], axes, backward)
    padded = jnp.concatenate([low, raw, high], axis=1)
    channels, rows, cols = padded.shape
    grid = padded.reshape(channels, rows, cols // PATCH, PATCH).transpose(2, 0, 1, 3)
    left = jnp.pad(grid[:-1, :, :, -1:], ((1, 0), (0, 0), (0, 0), (0, 0)))
    right = jnp.pad(grid[1:, :, :, :1], ((0, 1), (0, 0), (0, 0), (0, 0)))
    return jnp.concatenate([left, grid, right], axis=3).reshape(cols // PATCH, -1)


def spread_of(stem):
    return (
        lax.broadcasted_iota(jnp.int32, (stem, stem * CLASSES), 0)
        == lax.broadcasted_iota(jnp.int32, (stem, stem * CLASSES), 1) // CLASSES
    )


def front_kernel(
    win_ref, table_ref, taps_ref, embed_ref, gain_ref, router_ref, routes_ref, cot_ref,
    sent_ref, preact_ref, patches_ref, embedded_ref, inv_ref, hidden_ref, score_ref, slot_ref,
    winall_ref,
):
    tokens, width = cot_ref.shape
    experts, double, _ = sent_ref.shape
    cap = double // 2
    stem = taps_ref.shape[1]
    win_all = mm(win_ref[...], table_ref[...]).astype(BF)
    winall_ref[...] = win_all
    rep = mm(taps_ref[...], spread_of(stem).astype(BF))
    cls = lax.broadcasted_iota(jnp.int32, rep.shape, 1) % CLASSES
    kernel = jnp.concatenate([jnp.where(cls == q, rep, 0.0) for q in range(CLASSES)], axis=0)
    preact = mm(win_all, kernel.astype(BF))
    preact_ref[...] = preact
    tanh_v = jnp.tanh(GELU_C * (preact + GELU_A * preact * preact * preact))
    patches = (0.5 * preact * (1.0 + tanh_v)).astype(BF)
    patches_ref[...] = patches
    embedded = mm(patches, embed_ref[...])
    embedded_ref[...] = embedded
    inv = lax.rsqrt(jnp.mean(embedded * embedded, axis=-1, keepdims=True) + EPSILON)
    inv_ref[...] = inv
    hidden = (embedded * inv * gain_ref[...]).astype(BF)
    hidden_ref[...] = hidden
    logits = mm(hidden, router_ref[...])
    routes = routes_ref[...]
    hot = routes == lax.broadcasted_iota(jnp.int32, (tokens, experts), 1)
    score = jax.nn.sigmoid(jnp.sum(jnp.where(hot, logits, 0.0), axis=1, keepdims=True))
    score_ref[...] = score
    earlier = lax.broadcasted_iota(jnp.int32, (tokens, tokens), 1) < lax.broadcasted_iota(
        jnp.int32, (tokens, tokens), 0
    )
    before = mm(earlier.astype(BF), hot.astype(BF))
    pos = jnp.sum(jnp.where(hot, before, 0.0), axis=1, keepdims=True).astype(jnp.int32)
    slot = routes * cap + pos
    slot_ref[...] = slot
    select = (slot == lax.broadcasted_iota(jnp.int32, (tokens, experts * cap), 1)).astype(BF)
    out_cot = (score * cot_ref[...].astype(F32)).astype(BF)
    rows = mm(select, hidden, TN).reshape(experts, cap, width)
    cots = mm(select, out_cot, TN).reshape(experts, cap, width)
    sent_ref[...] = jnp.concatenate([rows, cots], axis=1).astype(BF)


def greet(devices):
    barrier = pltpu.get_barrier_semaphore()
    for device in devices:
        pl.semaphore_signal(barrier, inc=1, device_id=device, device_id_type=MESH)
    pl.semaphore_wait(barrier, len(devices))


def expert_kernel(
    sent_ref, gate_ref, up_ref, down_ref,
    ret_ref, ggate_ref, gup_ref, gdown_ref,
    wg, wu, wd, grp, part, rx1, tx2, rx2, fin, rows_all, cots_all, act_all, gcot_all, ucot_all,
    stage, load_sem, own_sem, store_sem, send_sem, recv_sem,
):
    count, members, double, width = grp.shape
    cap = double // 2
    share = wg.shape[1]
    me_e, me_t = lax.axis_index("de"), lax.axis_index("tp")
    total = count * members * cap
    batch = 256
    per = batch // (members * cap)
    steps = count // per
    loads = [
        pltpu.make_async_copy(src, dst, load_sem.at[i])
        for i, (src, dst) in enumerate(
            ((gate_ref.at[0], wg), (up_ref.at[0], wu), (down_ref.at[0], wd))
        )
    ]
    for load in loads:
        load.start()

    def remote(kind, k, src, dst, device):
        return pltpu.make_async_remote_copy(
            src_ref=src, dst_ref=dst, send_sem=send_sem.at[kind, k], recv_sem=recv_sem.at[kind, k],
            device_id=device, device_id_type=MESH,
        )

    near, far = (me_e, me_t ^ 1), (me_e, me_t ^ 2)
    a2a = lambda k: remote(0, k, sent_ref.at[me_e ^ k], grp.at[k, 0], (me_e ^ k, me_t))
    to_near = lambda k: remote(1, k, grp.at[k, 0], grp.at[k, 1], near)
    to_far = lambda k: remote(2, k, grp.at[k, 0], grp.at[k, 2], far)
    pass_near = lambda k: remote(3, k, grp.at[k, 2], grp.at[k, 3], near)
    sum_near_a = lambda k: remote(4, k, part.at[k, 1], rx1.at[k, 0], near)
    sum_near_b = lambda k: remote(5, k, part.at[k, 3], rx1.at[k, 1], near)
    sum_far = lambda k: remote(6, k, tx2.at[k], rx2.at[k], far)
    back = lambda k: remote(7, k, fin.at[k], ret_ref.at[me_e], (me_e ^ k, me_t))

    greet([(me_e ^ k, me_t) for k in range(1, count)] + [near, far])
    for k in range(1, count):
        a2a(k).start()
    own = pltpu.make_async_copy(sent_ref.at[me_e], grp.at[0, 0], own_sem)
    own.start()
    own.wait()

    def forward(p):
        for i in range(per):
            k = p * per + i

            @pl.when(k > 0)
            def _():
                a2a(k).wait_recv()

            to_far(k).start()
            to_near(k).start()

    def arrive(p):
        for i in range(per):
            k = p * per + i
            to_far(k).wait_recv()
            pass_near(k).start()
        for i in range(per):
            k = p * per + i
            to_near(k).wait_recv()
            pass_near(k).wait_recv()

    def gather(p):
        blocks = grp[pl.ds(p * per, per)]
        if cap % 16:
            blocks = blocks.astype(F32)
        rows = blocks[:, :, :cap].reshape(batch, width).astype(BF)
        cots = blocks[:, :, cap:].reshape(batch, width).astype(BF)
        at = pl.ds(pl.multiple_of(p * batch, batch), batch)
        rows_all[at, :] = rows
        cots_all[at, :] = cots

    tile = 256

    def compute(p):
        at = pl.ds(pl.multiple_of(p * batch, batch), batch)

        @pl.loop(0, share // tile)
        def _(f):
            cols = pl.ds(pl.multiple_of(f * tile, tile), tile)
            gate = mm(rows_all[at, :], wg[:, cols])
            up = mm(rows_all[at, :], wu[:, cols])
            act_cot = mm(cots_all[at, :], wd[cols, :], NT)
            sig = jax.nn.sigmoid(gate)
            activated = gate * sig
            act_all[at, cols] = (activated * up).astype(BF)
            gcot_all[at, cols] = (act_cot * up * (sig * (1.0 + gate * (1.0 - sig)))).astype(BF)
            ucot_all[at, cols] = (act_cot * activated).astype(BF)

        @pl.loop(0, width // tile)
        def _(x):
            cols = pl.ds(pl.multiple_of(x * tile, tile), tile)
            out = mm(act_all[at, :], wd[:, cols])
            back_cot = mm(gcot_all[at, :], wg[cols, :], NT) + mm(ucot_all[at, :], wu[cols, :], NT)
            both = jnp.concatenate(
                [out.reshape(per, members, cap, tile), back_cot.reshape(per, members, cap, tile)],
                axis=2,
            )
            part[pl.ds(p * per, per), :, :, cols] = both.astype(BF)

    def reduce_near(p):
        for i in range(per):
            k = p * per + i
            sum_near_a(k).wait_recv()
            sum_near_b(k).wait_recv()
            tx2[k] = (part[k, 2].astype(F32) + rx1[k, 1].astype(F32)).astype(BF)
            sum_far(k).start()

    def reduce_far(p):
        for i in range(per):
            k = p * per + i
            sum_far(k).wait_recv()
            fin[k] = (
                part[k, 0].astype(F32) + rx1[k, 0].astype(F32) + rx2[k].astype(F32)
            ).astype(BF)

            @pl.when(k > 0)
            def _():
                back(k).start()

    forward(0)
    for load in loads:
        load.wait()

    @pl.loop(0, steps)
    def _(p):
        @pl.when(p < steps - 1)
        def _():
            forward(p + 1)

        arrive(p)
        gather(p)
        compute(p)
        for i in range(per):
            k = p * per + i
            sum_near_a(k).start()
            sum_near_b(k).start()

        @pl.when(p >= 1)
        def _():
            reduce_near(p - 1)

        @pl.when(p >= 2)
        def _():
            reduce_far(p - 2)

    half = 256

    def grads(j, lhs, rhs, out_ref):
        n = width // half

        def piece(c):
            return pltpu.make_async_copy(
                stage.at[j], out_ref.at[0, pl.ds(pl.multiple_of(c * half, half), half), :],
                store_sem.at[j],
            )

        @pl.loop(0, n)
        def _(c):
            @pl.when(c > 0)
            def _():
                piece(c - 1).wait()

            at = pl.ds(pl.multiple_of(c * half, half), half)
            stage[j] = mm(lhs[:, at], rhs[...], TN)
            piece(c).start()

        return lambda: piece(n - 1).wait()

    ends = [grads(0, rows_all, gcot_all, ggate_ref)]
    reduce_near(steps - 1)
    if steps >= 2:
        reduce_far(steps - 2)
    ends.append(grads(1, rows_all, ucot_all, gup_ref))
    reduce_far(steps - 1)
    own_back = pltpu.make_async_copy(fin.at[0], ret_ref.at[me_e], own_sem)
    own_back.start()
    ends.append(grads(2, act_all, cots_all, gdown_ref))
    own_back.wait()
    for end in ends:
        end()
    for k in range(1, count):
        pltpu.make_async_remote_copy(
            src_ref=fin.at[k], dst_ref=ret_ref.at[me_e ^ k], send_sem=send_sem.at[7, k],
            recv_sem=recv_sem.at[7, k], device_id=(me_e ^ k, me_t), device_id_type=MESH,
        ).wait_recv()

    for k in range(count):
        if k:
            a2a(k).wait_send()
            back(k).wait_send()
        for copy in (to_near, to_far, pass_near, sum_near_a, sum_near_b, sum_far):
            copy(k).wait_send()


def token_kernel(
    ret_ref, slot_ref, routes_ref, score_ref, cot_ref, hidden_ref, embedded_ref, inv_ref, gain_ref,
    patches_ref, embed_ref, router_ref, preact_ref, winall_ref,
    mix_ref, big_ref, small_ref,
    eb, e_rx1, e_acc1, e_rx2, e_acc2, e_rx3, e_piece,
    sb, s_rx1, s_acc1, s_rx2, s_rx3, send_sem, recv_sem, own_sem,
):
    tokens, width = cot_ref.shape
    experts, double, _ = ret_ref.shape
    cap = double // 2
    chunks, patch_dim, lanes = eb.shape
    z_count = e_rx3.shape[0]
    piece = patch_dim // z_count
    me_e, me_t = lax.axis_index("de"), lax.axis_index("tp")
    b, g, z = me_t & 1, (me_t >> 1) * 2 + (me_e & 1), me_e >> 1
    near = (me_e, me_t ^ 1)
    cross = [None] + [(me_e ^ (r & 1), me_t ^ (r & 2)) for r in range(1, 4)]
    along = [None] + [(me_e ^ (2 * r), me_t) for r in range(1, z_count)]
    greet([near] + cross[1:] + along[1:])

    ret = ret_ref[...]
    if cap % 16:
        ret = ret.astype(F32)
    out_flat = ret[:, :cap].reshape(experts * cap, width).astype(BF)
    cot_flat = ret[:, cap:].reshape(experts * cap, width).astype(BF)
    select = (
        slot_ref[...] == lax.broadcasted_iota(jnp.int32, (tokens, experts * cap), 1)
    ).astype(BF)
    score = score_ref[...]
    out_wide = mm(select, out_flat)
    mix_ref[...] = (score * out_wide).astype(BF)
    score_grad = jnp.sum(cot_ref[...].astype(F32) * out_wide, axis=1, keepdims=True)
    local_grad = score_grad * score * (1.0 - score)
    hot = routes_ref[...] == lax.broadcasted_iota(jnp.int32, (tokens, experts), 1)
    logit_cot = jnp.where(hot, local_grad, 0.0).astype(BF)
    router_part = mm(logit_cot, hidden_ref[...], TN)
    upstream = mm(select, cot_flat) + mm(logit_cot, router_ref[...], NT)
    inv = inv_ref[...]
    normed = embedded_ref[...] * inv
    scaled = upstream * gain_ref[...]
    embed_cot = (
        inv * (scaled - normed * jnp.mean(scaled * normed, axis=1, keepdims=True))
    ).astype(BF)
    gain_part = jnp.sum(upstream * normed, axis=0, keepdims=True)
    patches = patches_ref[...]
    for c in range(0, chunks, 2):
        both = mm(patches, embed_cot[:, c * lanes : (c + 2) * lanes], TN).astype(BF)
        eb[c] = both[:, :lanes]
        eb[c + 1] = both[:, lanes:]

    def remote(kind, k, src, dst, device):
        return pltpu.make_async_remote_copy(
            src_ref=src, dst_ref=dst, send_sem=send_sem.at[kind, k], recv_sem=recv_sem.at[kind, k],
            device_id=device, device_id_type=MESH,
        )

    sent = []

    def send(*args):
        copy = remote(*args)
        copy.start()
        sent.append(copy)

    other = pl.ds((1 - b) * 4, 4)
    mine = pl.ds(b * 4, 4)
    send(0, 0, eb.at[other], e_rx1, near)

    preact = preact_ref[...]
    patch_cot = mm(embed_cot, embed_ref[...], NT)
    tanh_v = jnp.tanh(GELU_C * (preact + GELU_A * preact * preact * preact))
    slope = 0.5 * (1.0 + tanh_v) + 0.5 * preact * (1.0 - tanh_v * tanh_v) * GELU_C * (
        1.0 + 3.0 * GELU_A * preact * preact
    )
    preact_cot = (patch_cot * slope).astype(BF)
    cls = lax.broadcasted_iota(jnp.int32, (TAPS, patch_dim), 1) % CLASSES
    taps_all = mm(winall_ref[...], preact_cot, TN)
    taps = jnp.zeros((TAPS, patch_dim), F32)
    for q in range(CLASSES):
        taps = taps + jnp.where(cls == q, taps_all[q * TAPS : (q + 1) * TAPS], 0.0)
    stem = patch_dim // CLASSES
    stem_part = mm(taps, spread_of(stem).astype(F32), NT, lax.Precision.HIGHEST)
    stem_part = jnp.concatenate([stem_part, jnp.zeros((TAPS, lanes - stem), F32)], axis=1)
    gain_rows = jnp.broadcast_to(gain_part, (8, width))
    for c in range(chunks):
        at = slice(c * lanes, (c + 1) * lanes)
        sb[c, :experts] = router_part[:, at]
        sb[c, experts : experts + 8] = gain_rows[:, at]
        sb[c, experts + 8 :] = (
            stem_part[c * 8 : c * 8 + 8] if c * 8 < TAPS else jnp.zeros((8, lanes), F32)
        )
    send(1, 0, sb.at[other], s_rx1, near)

    remote(0, 0, eb.at[other], e_rx1, near).wait_recv()
    for c in range(4):
        e_acc1[c] = (eb[b * 4 + c].astype(F32) + e_rx1[c].astype(F32)).astype(BF)
    for r in range(1, 4):
        send(2, r, e_acc1.at[g ^ r], e_rx2.at[r], cross[r])
    remote(1, 0, sb.at[other], s_rx1, near).wait_recv()
    for c in range(4):
        s_acc1[c] = sb[b * 4 + c] + s_rx1[c]
    for r in range(1, 4):
        send(3, r, s_acc1.at[g ^ r], s_rx2.at[r], cross[r])
    for r in range(1, 4):
        remote(2, r, e_acc1.at[g ^ r], e_rx2.at[r], cross[r]).wait_recv()
    e_acc2[...] = (
        e_acc1[g].astype(F32) + e_rx2[1].astype(F32) + e_rx2[2].astype(F32) + e_rx2[3].astype(F32)
    ).astype(BF)
    rows_of = lambda i: pl.ds(pl.multiple_of(i * piece, piece), piece)
    for r in range(1, z_count):
        send(4, r, e_acc2.at[rows_of(z ^ r)], e_rx3.at[r], along[r])
    for r in range(1, 4):
        remote(3, r, s_acc1.at[g ^ r], s_rx2.at[r], cross[r]).wait_recv()
    s_rx3[z] = s_acc1[g] + s_rx2[1] + s_rx2[2] + s_rx2[3]
    for r in range(1, z_count):
        send(5, r, s_rx3.at[z], s_rx3.at[z], along[r])
    total = e_acc2[rows_of(z), :].astype(F32)
    for r in range(1, z_count):
        remote(4, r, e_acc2.at[rows_of(z ^ r)], e_rx3.at[r], along[r]).wait_recv()
        total = total + e_rx3[r].astype(F32)
    e_piece[...] = total.astype(BF)
    own = b * 4 + g
    for r in range(1, z_count):
        send(6, r, e_piece, big_ref.at[own, rows_of(z)], along[r])
    big_ref[own, rows_of(z), :] = total.astype(BF)
    for r in range(1, z_count):
        remote(5, r, s_rx3.at[z], s_rx3.at[z ^ r], along[r]).wait_recv()
    s_total = s_rx3[0]
    for i in range(1, z_count):
        s_total = s_total + s_rx3[i]
    small_ref[own] = s_total
    for r in range(1, 4):
        send(7, r, small_ref.at[own], small_ref.at[own], cross[r])
    for r in range(1, z_count):
        remote(6, r, e_piece, big_ref.at[own, rows_of(z ^ r)], along[r]).wait_recv()
    for r in range(1, 4):
        send(8, r, big_ref.at[own], big_ref.at[own], cross[r])
    for r in range(1, 4):
        remote(7, r, small_ref.at[own], small_ref.at[b * 4 + (g ^ r)], cross[r]).wait_recv()
    send(9, 0, small_ref.at[mine], small_ref.at[mine], near)
    send(10, 0, big_ref.at[own], big_ref.at[own], near)
    for r in range(1, 4):
        theirs = b * 4 + (g ^ r)
        remote(8, r, big_ref.at[own], big_ref.at[theirs], cross[r]).wait_recv()
        send(10, r, big_ref.at[theirs], big_ref.at[theirs], near)
    remote(9, 0, small_ref.at[mine], small_ref.at[other], near).wait_recv()
    for r in range(4):
        theirs = (1 - b) * 4 + (g ^ r)
        remote(10, r, big_ref.at[theirs], big_ref.at[theirs], near).wait_recv()
    for copy in sent:
        copy.wait_send()


def local(
    raw_tiles, stem_weight, embed_weight, norm_gain, router_weight, w_gate, w_up, w_down, routes,
    cotangent,
):
    tokens, width = cotangent.shape
    owners, members = lax.axis_size("de"), lax.axis_size("tp")
    experts = w_gate.shape[0] * owners
    cap = 2 * tokens // experts
    share = w_gate.shape[2]
    channels = raw_tiles.shape[0]
    stem = stem_weight.shape[0]
    patch_dim = embed_weight.shape[0]
    total = owners * members * cap
    shape = jax.ShapeDtypeStruct
    win = windows(raw_tiles)
    table = jnp.asarray(tap_table(channels), BF)
    taps = jnp.pad(stem_weight.reshape(stem, channels * 9).T, ((0, TAPS - channels * 9), (0, 0)))
    gain = norm_gain.reshape(1, width)
    sent, preact, patches, embedded, inv, hidden, score, slot, winall = pl.pallas_call(
        front_kernel,
        out_shape=(
            shape((experts, 2 * cap, width), BF),
            shape((tokens, patch_dim), F32),
            shape((tokens, patch_dim), BF),
            shape((tokens, width), F32),
            shape((tokens, 1), F32),
            shape((tokens, width), BF),
            shape((tokens, 1), F32),
            shape((tokens, 1), jnp.int32),
            shape((tokens, CLASSES * TAPS), BF),
        ),
        in_specs=[VMEM] * 8,
        out_specs=(VMEM,) * 9,
        compiler_params=pltpu.CompilerParams(vmem_limit_bytes=32 << 20),
        name="front",
    )(win, table, taps, embed_weight, gain, router_weight, routes, cotangent)

    anywhere = pl.BlockSpec(memory_space=pl.ANY)
    block = (2 * cap, width)
    ret, grad_gate, grad_up, grad_down = pl.pallas_call(
        expert_kernel,
        out_shape=(
            shape((experts,) + block, BF),
            shape(w_gate.shape, F32),
            shape(w_up.shape, F32),
            shape(w_down.shape, F32),
        ),
        in_specs=[VMEM] + [anywhere] * 3,
        out_specs=(VMEM,) + (anywhere,) * 3,
        scratch_shapes=[
            pltpu.VMEM((width, share), BF),
            pltpu.VMEM((width, share), BF),
            pltpu.VMEM((share, width), BF),
            pltpu.VMEM((owners, members) + block, BF),
            pltpu.VMEM((owners, members) + block, BF),
            pltpu.VMEM((owners, 2) + block, BF),
            pltpu.VMEM((owners,) + block, BF),
            pltpu.VMEM((owners,) + block, BF),
            pltpu.VMEM((owners,) + block, BF),
            pltpu.VMEM((total, width), BF),
            pltpu.VMEM((total, width), BF),
            pltpu.VMEM((total, share), BF),
            pltpu.VMEM((total, share), BF),
            pltpu.VMEM((total, share), BF),
            pltpu.VMEM((3, 256, width), F32),
            pltpu.SemaphoreType.DMA((3,)),
            pltpu.SemaphoreType.DMA,
            pltpu.SemaphoreType.DMA((3,)),
            pltpu.SemaphoreType.DMA((8, owners)),
            pltpu.SemaphoreType.DMA((8, owners)),
        ],
        compiler_params=pltpu.CompilerParams(
            vmem_limit_bytes=56 << 20, collective_id=1, has_side_effects=True
        ),
        name="experts",
    )(sent, w_gate, w_up, w_down)

    lanes = width // 8
    z_count = owners // 2
    small_rows = experts + 16
    mix, big, small = pl.pallas_call(
        token_kernel,
        out_shape=(
            shape((tokens, width), BF),
            shape((8, patch_dim, lanes), BF),
            shape((8, small_rows, lanes), F32),
        ),
        in_specs=[VMEM] * 14,
        out_specs=(VMEM,) * 3,
        scratch_shapes=[
            pltpu.VMEM((8, patch_dim, lanes), BF),
            pltpu.VMEM((4, patch_dim, lanes), BF),
            pltpu.VMEM((4, patch_dim, lanes), BF),
            pltpu.VMEM((4, patch_dim, lanes), BF),
            pltpu.VMEM((patch_dim, lanes), BF),
            pltpu.VMEM((z_count, patch_dim // z_count, lanes), BF),
            pltpu.VMEM((patch_dim // z_count, lanes), BF),
            pltpu.VMEM((8, small_rows, lanes), F32),
            pltpu.VMEM((4, small_rows, lanes), F32),
            pltpu.VMEM((4, small_rows, lanes), F32),
            pltpu.VMEM((4, small_rows, lanes), F32),
            pltpu.VMEM((z_count, small_rows, lanes), F32),
            pltpu.SemaphoreType.DMA((11, max(4, z_count))),
            pltpu.SemaphoreType.DMA((11, max(4, z_count))),
            pltpu.SemaphoreType.DMA,
        ],
        compiler_params=pltpu.CompilerParams(
            vmem_limit_bytes=40 << 20, collective_id=2, has_side_effects=True
        ),
        name="tokens",
    )(
        ret, slot, routes, score, cotangent, hidden, embedded, inv, gain, patches, embed_weight,
        router_weight, preact, winall,
    )
    grad_embed = big.transpose(1, 0, 2).reshape(patch_dim, width).astype(F32)
    grad_router = small[:, :experts].transpose(0, 2, 1).reshape(width, experts)
    grad_gain = small[:, experts].reshape(width)
    taps_grad = small[: TAPS // 8, experts + 8 :].reshape(TAPS, lanes)[: channels * 9, :stem]
    return (
        mix, grad_gate, grad_up, grad_down, grad_router, grad_gain, grad_embed,
        taps_grad.T.reshape(stem_weight.shape),
    )


def solution(mesh):
    tiles = P(("de", "tp"), None)
    columns, rows = P("de", None, "tp"), P("de", "tp", None)
    return jax.shard_map(
        local,
        mesh=mesh,
        in_specs=(
            P(None, ("de", "tp"), None), P(), P(), P(), P(), columns, columns, rows, tiles, tiles,
        ),
        out_specs=(tiles, columns, columns, rows, P(), P(), P(), P()),
        check_vma=False,
    )
```

time: 424 us -> 165 us (0.39)
  waiting for transfers between devices: 232 us -> 0.01 us
  Pallas kernels: 0 us -> 125 us
  blocking collectives: 81.1 us -> 0 us
  matrix products: 56.5 us -> 0 us
  local copies, waits for them, and re-layouts: 13.3 us -> 29.4 us
  between operations: 14.2 us -> 0.83 us
  starting transfers between devices: 15.3 us -> 4.32 us
  other arithmetic: 11.3 us -> 4.45 us
    pallas_call x0 -> x3, Pallas kernels: none -> 125 us  [the longest x1 79.5 us: local(): pl.pallas_call(expert_kernel, out_shape=(shape((experts,) + block, BF), s...]
    psum x1 -> x0, waiting for transfers between devices: 86.7 us -> none  [local(): lax.psum((gain_part, embed_part, stem_part), ('de', 'tp'))]
    reduce_scatter x2 -> x0, waiting for transfers between devices: 80.2 us -> none  [collect(): lax.psum_scatter(partial_term(jnp.int32(0), total_rows // members * lax.a...]
    dot_general x19 -> x0, matrix products: 56.5 us -> none  [the longest x1 6.98 us: local(): jnp.einsum('tslcf,tslcx->lfx', hidden_act, group_cots, preferred_element_...]
    all_gather x2 -> x0, waiting for transfers between devices: 43.1 us -> none  [dispatch(): return lax.all_gather(moved[None], 'tp', axis=0, tiled=True)]
    all_to_all x2 -> x0, blocking collectives: 41.1 us -> none  [dispatch(): lax.all_to_all(buffer, 'de', split_axis=0, concat_axis=0, tiled=True)]
    psum x1 -> x0, blocking collectives: 40 us -> none  [local(): router_total = lax.psum(router_part, ('de', 'tp'))]
    all_to_all x2 -> x0, waiting for transfers between devices: 20.8 us -> none  [collect(): lax.all_to_all(share_b, 'de', split_axis=0, concat_axis=0, tiled=True)]
  transfers between devices with their start and end apart: 9 -> 2, of which waited for: 8 -> 0; matrix products, arithmetic and copies ran while one was open for 7% -> 1% of each run, Pallas kernels for 0% -> 0%
where the time goes in v1:
time: 165 us; the launch traced here: 164 us
  Pallas kernels  125 us (76%)
  local copies, waits for them, and re-layouts  29.4 us (18%)
  other arithmetic  4.45 us (3%)
  starting transfers between devices  4.32 us (3%)
    pallas_call x1, Pallas kernels, local(): pl.pallas_call(expert_kernel, out_shape=(shape((experts,) + block, BF), s...  79.5 us
    pallas_call x1, Pallas kernels, local(): pl.pallas_call(token_kernel, out_shape=(shape((tokens, width), BF), shape...  43.5 us
    unnamed x25, local copies, waits for them, and re-layouts  20.1 us
    convert_element_type x1, local copies, waits for them, and re-layouts, local(): grad_embed = big.transpose(1, 0, 2).reshape(patch_dim, width).astype(F32)  3.54 us
  transfers between devices with their start and end apart: 2, of which 0 were waited for; matrix products, arithmetic and copies ran while one was open for 1% of the time, Pallas kernels for 0%

profile of v1, /device:TPU:0, one launch (start us, length us, event | category | flops | bytes accessed | tf_op | source)
XLA Modules:
  0.0 163.8 jit_solution(2598087331684355975)
XLA Ops:
  0.6 0.8 fusion.5
  1.4 1.3 collective-permute-start.1
  2.7 3.0 %collective-permute-start = (bf16[4,1,512]{2,1,0:T(2,128)(2,1)S(1)}, bf16[4,1,512]{2,1,0:T(2,128)(2,1)S(1)}, u32[]{:S(2)}, u32[]{:S(2)}) collective-permute-start(bf16[4,1,512]{2,1,0:T(2,128)(2,1)S(1)} %get-tuple-element.66), channel_id=1, source_target_pairs={{0,1},{1,2},{2,3},{3,4},{4,5},{5,6},{6,7},{7,8},{8,9},{9,10},{10,1... | collective-permute-start | bytes 12296 | tf_op jit(solution)/shard_map/ppermute | solution.py:46
  5.8 0.7 copy.52
  6.5 0.9 copy.54.router_ref
  7.4 0.8 copy.55.routes_ref
  8.2 0.8 pad_maximum_fusion
  9.0 1.7 %reshape.40 = bf16[4,6,128,4]{3,2,0,1:T(8,128)(2,1)S(1)} reshape(bf16[4,6,512]{2,0,1:T(4,128)(2,1)S(1)} %copy.50) | data formatting | bytes 49152 | tf_op jit(solution)/shard_map/reshape | solution.py:50
  10.6 0.5 fusion.4
  11.2 0.0 copy-start
  11.2 0.0 copy-start.3
  11.2 0.0 copy-start.4
  11.2 0.0 copy-start.5
  11.2 1.8 %fusion.2 = bf16[128,4,6,6]{3,0,1,2:T(8,128)(2,1)} fusion(bf16[127,4,6,1]{3,0,1,2:T(8,128)(2,1)S(1)} %get-tuple-element.65, bf16[127,4,6,1]{3,0,1,2:T(8,128)(2,1)S(1)} %get-tuple-element.64, bf16[128,4,6,4]{3,0,1,2:T(8,128)(2,1)S(1)} %bitcast.27), kind=kLoop, calls=%fused_computation.5 | loop fusion | flops 184320 | bytes 73632 | tf_op jit(solution)/shard_map/concatenate | solution.py:53
  13.0 1.4 copy.51
  14.5 0.1 copy.53.win_ref
  14.7 1.8 %front.1 = (bf16[8,64,1024]{2,1,0:T(8,128)(2,1)S(1)}, f32[128,768]{1,0:T(8,128)S(1)}, bf16[128,768]{1,0:T(8,128)(2,1)S(1)}, f32[128,1024]{1,0:T(8,128)S(1)}, f32...) custom-call(bf16[128,144]{1,0:T(8,128)(2,1)S(1)} %copy.53.win_ref, ...), custom_call_target="tpu_custom_call" | custom-call | tf_op jit(solution)/shard_map/front/pallas_call | solution.py:484
  16.5 1.0 copy-done.1
  17.4 79.5 %experts.1 = (bf16[8,64,1024]{2,1,0:T(8,128)(2,1)}, f32[1,1024,1024]{2,1,0:T(8,128)}, f32[1,1024,1024]{2,1,0:T(8,128)}, f32[1,1024,1024]{2,1,0:T(8,128)}) custom-call(bf16[8,64,1024]{2,1,0:T(8,128)(2,1)} %copy-done.1, bf16[1,1024,1024]{2,1,0:T(8,128)(2,1)} %gate_ref.1, bf16[1,1024,1024]{2,1,0:T(8,128)(2,1)} %up_ref.1, bf16[1,1024,1024]{2,1,0:T(8,128)(2,1)} %down_ref.1), custom_call_target="tpu_custom_call" | custom-call | tf_op jit(solution)/shard_map/experts/pallas_call | solution.py:505
  96.9 1.2 copy-done.2
  98.1 43.5 %tokens.1 = (bf16[128,1024]{1,0:T(8,128)(2,1)S(1)}, bf16[8,768,128]{2,1,0:T(8,128)(2,1)S(1)}, f32[8,24,128]{2,1,0:T(8,128)S(1)}) custom-call(bf16[8,64,1024]{2,1,0:T(8,128)(2,1)S(1)} %copy-done.2, s32[128,1]{1,0:T(8,128)S(1)} %get-tuple-element.26.slot_ref, s32[128,1]{1,0:T(8,128)S(1)} %copy.55.routes_ref, f32[128,1]{1,0:T(8,128)S(1)} %get-tuple-element.27.score_ref, ...), custom_call_target="tpu_custom_call" | custom-call | tf_op jit(solution)/shard_map/tokens/pallas_call | solution.py:546
  141.7 0.6 slice_bitcast_fusion
  142.3 0.6 slice.29
  142.9 1.9 %convert_bitcast_fusion = f32[768,8,128]{2,0,1:T(8,128)} fusion(bf16[8,768,128]{2,1,0:T(8,128)(2,1)S(1)} %get-tuple-element.39), kind=kLoop, calls=%fused_computation | loop fusion | flops 786432 | bytes 4718592 | tf_op jit(solution)/shard_map/convert_element_type | solution.py:580
  144.8 3.5 %copy.58 = f32[768,8,128]{0,2,1:T(8,128)} copy(f32[768,8,128]{2,0,1:T(8,128)} %convert_bitcast_fusion) | data formatting | bytes 6291456 | tf_op jit(solution)/shard_map/convert_element_type | solution.py:580
  148.3 3.5 %copy.59 = f32[768,1024]{1,0:T(8,128)} copy(f32[768,1024]{0,1:T(8,128)} %bitcast.25) | data formatting | bytes 6291456
  151.9 0.6 copy.60
  152.5 0.7 copy.65
  153.2 4.9 %copy.66 = f32[1,1024,1024]{2,1,0:T(8,128)} copy(f32[1,1024,1024]{2,1,0:T(8,128)} %get-tuple-element.77) | data formatting | bytes 8388608
  158.1 2.1 %copy.67 = f32[1,1024,1024]{2,1,0:T(8,128)} copy(f32[1,1024,1024]{2,1,0:T(8,128)S(1)} %copy-done.7) | data formatting | bytes 8388608
  160.2 1.6 copy-done.6
  161.8 2.0 %copy.68 = f32[1,1024,1024]{2,1,0:T(8,128)} copy(f32[1,1024,1024]{2,1,0:T(8,128)S(1)} %copy-done.6) | data formatting | bytes 8388608
  (18 shorter events, 0.1 us)
Async XLA Ops:
  1.4 6.7 %collective-permute-start.1 = (bf16[4,1,512]{2,1,0:T(2,128)(2,1)S(1)}, bf16[4,1,512]{2,1,0:T(2,128)(2,1)S(1)}, u32[]{:S(2)}, u32[]{:S(2)}) collective-permute-start(bf16[4,1,512]{2,1,0:T(2,128)(2,1)S(1)} %get-tuple-element.67), channel_id=1, source_target_pairs={{1,0},{2,1},{3,2},{4,3},{5,4},{6,5},{7,6},{8,7},{9,8},{10,9},{11,1... | collective-permute-start | bytes 12296 | tf_op jit(solution)/shard_map/ppermute | solution.py:47
  2.7 5.5 %collective-permute-start = (bf16[4,1,512]{2,1,0:T(2,128)(2,1)S(1)}, bf16[4,1,512]{2,1,0:T(2,128)(2,1)S(1)}, u32[]{:S(2)}, u32[]{:S(2)}) collective-permute-start(bf16[4,1,512]{2,1,0:T(2,128)(2,1)S(1)} %get-tuple-element.66), channel_id=1, source_target_pairs={{0,1},{1,2},{2,3},{3,4},{4,5},{5,6},{6,7},{7,8},{8,9},{9,10},{10,1... | collective-permute-start | bytes 12296 | tf_op jit(solution)/shard_map/ppermute | solution.py:46
  11.2 3.5 %copy-start = (bf16[768,1024]{1,0:T(8,128)(2,1)S(1)}, bf16[768,1024]{1,0:T(8,128)(2,1)}, u32[]{:S(2)}) copy-start(bf16[768,1024]{1,0:T(8,128)(2,1)} %embed_ref.3) | copy-start | bytes 4718596
  11.2 3.5 %copy-start.3 = (bf16[128,1024]{1,0:T(8,128)(2,1)S(1)}, bf16[128,1024]{1,0:T(8,128)(2,1)}, u32[]{:S(2)}) copy-start(bf16[128,1024]{1,0:T(8,128)(2,1)} %cot_ref.3) | copy-start | bytes 786436
  11.2 3.5 %copy-start.4 = (bf16[144,640]{1,0:T(8,128)(2,1)S(1)}, bf16[144,640]{1,0:T(8,128)(2,1)}, u32[]{:S(2)}) copy-start(bf16[144,640]{1,0:T(8,128)(2,1)} %constant.5.clone.table_ref) | copy-start | bytes 552964
  11.2 3.5 %copy-start.5 = (f32[1024]{0:T(1024)S(1)}, f32[1024]{0:T(1024)}, u32[]{:S(2)}) copy-start(f32[1024]{0:T(1024)} %param.14) | copy-start | bytes 12292
  16.5 1.0 copy-start.1
  96.9 1.2 copy-start.2
  153.2 4.9 %copy-start.7 = (f32[1,1024,1024]{2,1,0:T(8,128)S(1)}, f32[1,1024,1024]{2,1,0:T(8,128)}, u32[]{:S(2)}) copy-start(f32[1,1024,1024]{2,1,0:T(8,128)} %get-tuple-element.78) | copy-start | bytes 12582916
  158.1 3.7 %copy-start.6 = (f32[1,1024,1024]{2,1,0:T(8,128)S(1)}, f32[1,1024,1024]{2,1,0:T(8,128)}, u32[]{:S(2)}) copy-start(f32[1,1024,1024]{2,1,0:T(8,128)} %get-tuple-element.79) | copy-start | bytes 12582916

commit v2 on v1

v2 whole, which is shorter than its diff:
```python
import jax
import jax.numpy as jnp
import numpy as np
from jax import lax
from jax.experimental import pallas as pl
from jax.experimental.pallas import tpu as pltpu
from jax.sharding import PartitionSpec as P

PATCH = 4
GELU_C = 0.7978845608028654
GELU_A = 0.044715
EPSILON = 1e-06
TAPS = 40
CLASSES = PATCH * PATCH
MESH = pl.DeviceIdType.MESH
BF = jnp.bfloat16
F32 = jnp.float32
VMEM = pl.BlockSpec(memory_space=pltpu.VMEM)
NT = (((1,), (1,)), ((), ()))
TN = (((0,), (0,)), ((), ()))


def mm(a, b, dims=(((1,), (0,)), ((), ())), precision=None):
    return lax.dot_general(a, b, dims, preferred_element_type=F32, precision=precision)


def tap_table(channels):
    side = PATCH + 2
    table = np.zeros((side, channels * 8, CLASSES * TAPS), np.float32)
    for q in range(CLASSES):
        for i in range(channels):
            for a in range(3):
                for b in range(3):
                    table[q % PATCH + b, i * 8 + q // PATCH + a, q * TAPS + i * 9 + a * 3 + b] = 1.0
    return table.reshape(side * channels * 8, CLASSES * TAPS)


def spread_of(stem):
    return (
        lax.broadcasted_iota(jnp.int32, (stem, stem * CLASSES), 0)
        == lax.broadcasted_iota(jnp.int32, (stem, stem * CLASSES), 1) // CLASSES
    )


def greet(devices):
    barrier = pltpu.get_barrier_semaphore()
    for device in devices:
        pl.semaphore_signal(barrier, inc=1, device_id=device, device_id_type=MESH)
    pl.semaphore_wait(barrier, len(devices))


def step_kernel(
    raw_ref, taps_ref, gain_ref, router_ref, routes_ref, cot_ref,
    table_hbm, embed_hbm, gate_ref, up_ref, down_ref,
    mix_ref, big_ref, small_ref, ggate_ref, gup_ref, gdown_ref,
    table_ref, embed_ref, wg, wu, wd, halo, sent_r, sent_c, grp_r, grp_c, part, rx1, rx2, ret_ref,
    rows_all, cots_all, act_all, gcot_all, ucot_all, stage,
    preact_ref, patches_ref, embedded_ref, inv_ref, hidden_ref, score_ref, slot_ref, winall_ref,
    eb, e_rx1, e_acc1, e_rx2, e_acc2, e_rx3, e_piece, sb, s_rx1, s_acc1, s_rx2, s_rx3,
    load_sem, own_sem, store_sem, halo_send, halo_recv, send_sem, recv_sem, red_send, red_recv,
):
    count, members, cap, width = grp_c.shape
    tokens = cot_ref.shape[0]
    experts = count
    share = wg.shape[1]
    stem = taps_ref.shape[0]
    channels, strip, pixel_cols = raw_ref.shape
    me_e, me_t = lax.axis_index("de"), lax.axis_index("tp")
    batch = 256
    per = batch // (members * cap)
    steps = count // per
    chunks, patch_dim, lanes = eb.shape
    z_count = e_rx3.shape[0]
    piece = patch_dim // z_count
    b, g, z = me_t & 1, (me_t >> 1) * 2 + (me_e & 1), me_e >> 1
    near, far = (me_e, me_t ^ 1), (me_e, me_t ^ 2)
    cross = [None] + [(me_e ^ (r & 1), me_t ^ (r & 2)) for r in range(1, 4)]
    along = [None] + [(me_e ^ (2 * r), me_t) for r in range(1, z_count)]
    loads = [
        pltpu.make_async_copy(src, dst, load_sem.at[i])
        for i, (src, dst) in enumerate(
            (
                (table_hbm, table_ref), (embed_hbm, embed_ref), (gate_ref.at[0], wg),
                (up_ref.at[0], wu), (down_ref.at[0], wd),
            )
        )
    ]
    for load in loads:
        load.start()

    def remote(kind, k, src, dst, device):
        return pltpu.make_async_remote_copy(
            src_ref=src, dst_ref=dst, send_sem=send_sem.at[kind, k], recv_sem=recv_sem.at[kind, k],
            device_id=device, device_id_type=MESH,
        )

    def moves(base, sent_ref, grp):
        return (
            lambda k: remote(base, k, sent_ref.at[me_e ^ k], grp.at[k, 0], (me_e ^ k, me_t)),
            lambda k: remote(base + 1, k, grp.at[k, 0], grp.at[k, 1], near),
            lambda k: remote(base + 2, k, grp.at[k, 0], grp.at[k, 2], far),
            lambda k: remote(base + 3, k, grp.at[k, 2], grp.at[k, 3], near),
        )

    rows_moves = moves(0, sent_r, grp_r)
    cots_moves = moves(4, sent_c, grp_c)
    sum_near_a = lambda k: remote(8, k, part.at[k, 1], rx1.at[k, 0], near)
    sum_near_b = lambda k: remote(9, k, part.at[k, 3], rx1.at[k, 1], near)
    sum_far = lambda k: remote(10, k, part.at[k, 2], rx2.at[k], far)
    back = lambda k: remote(11, k, part.at[k, 0], ret_ref.at[me_e], (me_e ^ k, me_t))
    back_in = lambda k: remote(11, k, part.at[k, 0], ret_ref.at[me_e ^ k], (me_e ^ k, me_t))

    place = me_e * members + me_t
    last = count * members - 1
    above = lax.rem(place + last, last + 1)
    below = lax.rem(place + 1, last + 1)
    strips = [
        pltpu.make_async_remote_copy(
            src_ref=raw_ref, dst_ref=halo.at[i], send_sem=halo_send.at[i], recv_sem=halo_recv.at[i],
            device_id=(to // members, lax.rem(to, members)), device_id_type=MESH,
        )
        for i, to in enumerate((below, above))
    ]
    greet(
        [(me_e ^ k, me_t) for k in range(1, count)]
        + [near, far, cross[3]]
        + [(to // members, lax.rem(to, members)) for to in (below, above)]
    )
    for strip_copy in strips:
        strip_copy.start()

    routes = routes_ref[...]
    hot = routes == lax.broadcasted_iota(jnp.int32, (tokens, experts), 1)
    earlier = lax.broadcasted_iota(jnp.int32, (tokens, tokens), 1) < lax.broadcasted_iota(
        jnp.int32, (tokens, tokens), 0
    )
    before = mm(earlier.astype(BF), hot.astype(BF))
    pos = jnp.sum(jnp.where(hot, before, 0.0), axis=1, keepdims=True).astype(jnp.int32)
    slot_ref[...] = routes * cap + pos

    def selector():
        return (
            slot_ref[...] == lax.broadcasted_iota(jnp.int32, (tokens, experts * cap), 1)
        ).astype(BF)

    def scatter(values, sent_ref, grp, move):
        sent_ref[...] = mm(selector(), values, TN).reshape(sent_ref.shape).astype(BF)
        for k in range(1, count):
            move[0](k).start()
        own = pltpu.make_async_copy(sent_ref.at[me_e], grp.at[0, 0], own_sem)
        own.start()
        own.wait()
        move[2](0).start()
        move[1](0).start()

    scatter(cot_ref[...], sent_c, grp_c, cots_moves)

    for strip_copy in strips:
        strip_copy.wait_recv()
    low = jnp.where(place > 0, halo[0].astype(F32), 0.0)
    high = jnp.where(place < last, halo[1].astype(F32), 0.0)
    raw = raw_ref[...].astype(F32)
    blank = jnp.zeros((8 - strip - 2, pixel_cols), F32)
    padded = jnp.concatenate(
        [
            part_rows
            for i in range(channels)
            for part_rows in (low[i, strip - 1 :], raw[i], high[i, :1], blank)
        ],
        axis=0,
    ).astype(BF)
    shape = (tokens, pixel_cols)
    token_of = lax.broadcasted_iota(jnp.int32, shape, 0)
    col_of = lax.broadcasted_iota(jnp.int32, shape, 1)
    pick = jnp.concatenate(
        [(col_of == token_of * PATCH + (dc - 1)).astype(F32) for dc in range(PATCH + 2)], axis=0
    ).astype(BF)
    picked = mm(pick, padded, NT)
    window = jnp.concatenate(
        [picked[dc * tokens : (dc + 1) * tokens] for dc in range(PATCH + 2)], axis=1
    ).astype(BF)
    loads[0].wait()
    win_all = mm(window, table_ref[...]).astype(BF)
    winall_ref[...] = win_all
    rep = mm(taps_ref[...], spread_of(stem).astype(BF), TN)
    cls = lax.broadcasted_iota(jnp.int32, rep.shape, 1) % CLASSES
    kernel = jnp.concatenate([jnp.where(cls == q, rep, 0.0) for q in range(CLASSES)], axis=0)
    preact = mm(win_all, kernel.astype(BF))
    preact_ref[...] = preact
    tanh_v = jnp.tanh(GELU_C * (preact + GELU_A * preact * preact * preact))
    patches = (0.5 * preact * (1.0 + tanh_v)).astype(BF)
    patches_ref[...] = patches
    loads[1].wait()
    embedded = mm(patches, embed_ref[...])
    embedded_ref[...] = embedded
    inv = lax.rsqrt(jnp.mean(embedded * embedded, axis=-1, keepdims=True) + EPSILON)
    inv_ref[...] = inv
    hidden = (embedded * inv * gain_ref[...]).astype(BF)
    hidden_ref[...] = hidden
    logits = mm(hidden, router_ref[...])
    score = jax.nn.sigmoid(jnp.sum(jnp.where(hot, logits, 0.0), axis=1, keepdims=True))
    score_ref[...] = score
    first = score.astype(BF).astype(F32)
    second = (score - first).astype(BF).astype(F32)
    third = score - first - second
    lane = lax.broadcasted_iota(jnp.int32, (tokens, 128), 1)
    tail = jnp.where(
        lane == 0, first, jnp.where(lane == 1, second, jnp.where(lane == 2, third, 0.0))
    )
    scatter(jnp.concatenate([hidden, tail.astype(BF)], axis=1), sent_r, grp_r, rows_moves)

    def forward(k, move):
        @pl.when(k > 0)
        def _():
            move[0](k).wait_recv()
            move[2](k).start()
            move[1](k).start()

    def forward_rows(p):
        for i in range(per):
            forward(p * per + i, rows_moves)

    def arrive(p, move):
        for i in range(per):
            k = p * per + i
            move[2](k).wait_recv()
            move[3](k).start()

    def settle(p, move):
        for i in range(per):
            k = p * per + i
            move[1](k).wait_recv()
            move[3](k).wait_recv()

    def flat(ref, p):
        blocks = ref[pl.ds(p * per, per)]
        if cap % 16:
            blocks = blocks.astype(F32)
        return blocks.reshape(batch, ref.shape[-1])

    def gather(p):
        at = pl.ds(pl.multiple_of(p * batch, batch), batch)
        rows = flat(grp_r, p)
        weight = jnp.sum(rows[:, width:].astype(F32), axis=1, keepdims=True)
        rows_all[at, :] = rows[:, :width].astype(BF)
        cots_all[at, :] = (weight * flat(grp_c, p).astype(F32)).astype(BF)

    tile = 256

    def compute(p):
        at = pl.ds(pl.multiple_of(p * batch, batch), batch)

        @pl.loop(0, share // tile)
        def _(f):
            cols = pl.ds(pl.multiple_of(f * tile, tile), tile)
            gate = mm(rows_all[at, :], wg[:, cols])
            up = mm(rows_all[at, :], wu[:, cols])
            act_cot = mm(cots_all[at, :], wd[cols, :], NT)
            sig = jax.nn.sigmoid(gate)
            activated = gate * sig
            act_all[at, cols] = (activated * up).astype(BF)
            gcot_all[at, cols] = (act_cot * up * (sig * (1.0 + gate * (1.0 - sig)))).astype(BF)
            ucot_all[at, cols] = (act_cot * activated).astype(BF)

        @pl.loop(0, width // tile)
        def _(x):
            cols = pl.ds(pl.multiple_of(x * tile, tile), tile)
            out = mm(act_all[at, :], wd[:, cols])
            back_cot = mm(gcot_all[at, :], wg[cols, :], NT) + mm(ucot_all[at, :], wu[cols, :], NT)
            both = jnp.concatenate(
                [out.reshape(per, members, cap, tile), back_cot.reshape(per, members, cap, tile)],
                axis=2,
            )
            part[pl.ds(p * per, per), :, :, cols] = both.astype(BF)

    def reduce_near(p):
        for i in range(per):
            k = p * per + i
            sum_near_a(k).wait_recv()
            sum_near_b(k).wait_recv()
            part[k, 2] = (part[k, 2].astype(F32) + rx1[k, 1].astype(F32)).astype(BF)
            sum_far(k).start()

    def reduce_far(p):
        for i in range(per):
            k = p * per + i
            sum_far(k).wait_recv()
            part[k, 0] = (
                part[k, 0].astype(F32) + rx1[k, 0].astype(F32) + rx2[k].astype(F32)
            ).astype(BF)

            @pl.when(k > 0)
            def _():
                back(k).start()

    @pl.loop(1, count)
    def _(k):
        forward(k, cots_moves)

    forward_rows(0)
    for load in loads[2:]:
        load.wait()

    @pl.loop(0, steps)
    def _(p):
        arrive(p, cots_moves)

        @pl.when(p < steps - 1)
        def _():
            forward_rows(p + 1)

        arrive(p, rows_moves)
        settle(p, cots_moves)
        settle(p, rows_moves)
        gather(p)
        compute(p)
        for i in range(per):
            k = p * per + i
            sum_near_a(k).start()
            sum_near_b(k).start()

        @pl.when(p >= 1)
        def _():
            reduce_near(p - 1)

        @pl.when(p >= 2)
        def _():
            reduce_far(p - 2)

    half = 256

    def grads(j, lhs, rhs, out_ref):
        n = width // half

        def store(c):
            return pltpu.make_async_copy(
                stage.at[j, c], out_ref.at[0, pl.ds(pl.multiple_of(c * half, half), half), :],
                store_sem.at[j, c],
            )

        @pl.loop(0, n)
        def _(c):
            at = pl.ds(pl.multiple_of(c * half, half), half)
            stage[j, c] = mm(lhs[:, at], rhs[...], TN)
            store(c).start()

        def finish():
            for c in range(n):
                store(c).wait()

        return finish

    reduce_near(steps - 1)
    if steps >= 2:
        reduce_far(steps - 2)
    ends = [grads(0, rows_all, gcot_all, ggate_ref)]
    reduce_far(steps - 1)
    own_back = pltpu.make_async_copy(part.at[0, 0], ret_ref.at[me_e], own_sem)
    own_back.start()
    ends.append(grads(1, rows_all, ucot_all, gup_ref))
    own_back.wait()
    for k in range(1, count):
        back_in(k).wait_recv()

    ret = ret_ref[...]
    if cap % 16:
        ret = ret.astype(F32)
    out_flat = ret[:, :cap].reshape(experts * cap, width).astype(BF)
    cot_flat = ret[:, cap:].reshape(experts * cap, width).astype(BF)
    select = selector()
    score = score_ref[...]
    out_wide = mm(select, out_flat)
    mix_ref[...] = (score * out_wide).astype(BF)
    score_grad = jnp.sum(cot_ref[...].astype(F32) * out_wide, axis=1, keepdims=True)
    local_grad = score_grad * score * (1.0 - score)
    hot = routes_ref[...] == lax.broadcasted_iota(jnp.int32, (tokens, experts), 1)
    logit_cot = jnp.where(hot, local_grad, 0.0).astype(BF)
    router_part = mm(logit_cot, hidden_ref[...], TN)
    upstream = mm(select, cot_flat) + mm(logit_cot, router_ref[...], NT)
    inv = inv_ref[...]
    normed = embedded_ref[...] * inv
    scaled = upstream * gain_ref[...]
    embed_cot = (
        inv * (scaled - normed * jnp.mean(scaled * normed, axis=1, keepdims=True))
    ).astype(BF)
    gain_part = jnp.sum(upstream * normed, axis=0, keepdims=True)
    patches = patches_ref[...]
    for c in range(0, chunks, 2):
        both = mm(patches, embed_cot[:, c * lanes : (c + 2) * lanes], TN).astype(BF)
        eb[c] = both[:, :lanes]
        eb[c + 1] = both[:, lanes:]

    def reduced(kind, k, src, dst, device):
        return pltpu.make_async_remote_copy(
            src_ref=src, dst_ref=dst, send_sem=red_send.at[kind, k], recv_sem=red_recv.at[kind, k],
            device_id=device, device_id_type=MESH,
        )

    sent = []

    def send(*args):
        copy = reduced(*args)
        copy.start()
        sent.append(copy)

    other = pl.ds((1 - b) * 4, 4)
    mine = pl.ds(b * 4, 4)
    send(0, 0, eb.at[other], e_rx1, near)

    preact = preact_ref[...]
    patch_cot = mm(embed_cot, embed_ref[...], NT)
    tanh_v = jnp.tanh(GELU_C * (preact + GELU_A * preact * preact * preact))
    slope = 0.5 * (1.0 + tanh_v) + 0.5 * preact * (1.0 - tanh_v * tanh_v) * GELU_C * (
        1.0 + 3.0 * GELU_A * preact * preact
    )
    preact_cot = (patch_cot * slope).astype(BF)
    cls = lax.broadcasted_iota(jnp.int32, (TAPS, patch_dim), 1) % CLASSES
    taps_all = mm(winall_ref[...], preact_cot, TN)
    taps = jnp.zeros((TAPS, patch_dim), F32)
    for q in range(CLASSES):
        taps = taps + jnp.where(cls == q, taps_all[q * TAPS : (q + 1) * TAPS], 0.0)
    stem_part = mm(spread_of(stem).astype(F32), taps, NT, lax.Precision.HIGHEST)
    stem_part = jnp.concatenate([stem_part, jnp.zeros((stem, lanes - TAPS), F32)], axis=1)
    gain_rows = jnp.broadcast_to(gain_part, (8, width))
    for c in range(chunks):
        at = slice(c * lanes, (c + 1) * lanes)
        sb[c, :experts] = router_part[:, at]
        sb[c, experts : experts + 8] = gain_rows[:, at]
        sb[c, experts + 8 :] = (
            stem_part[c * 8 : c * 8 + 8] if c * 8 < stem else jnp.zeros((8, lanes), F32)
        )
    send(1, 0, sb.at[other], s_rx1, near)

    reduced(0, 0, eb.at[other], e_rx1, near).wait_recv()
    for c in range(4):
        e_acc1[c] = (eb[b * 4 + c].astype(F32) + e_rx1[c].astype(F32)).astype(BF)
    for r in range(1, 4):
        send(2, r, e_acc1.at[g ^ r], e_rx2.at[r], cross[r])
    ends.append(grads(2, act_all, cots_all, gdown_ref))
    reduced(1, 0, sb.at[other], s_rx1, near).wait_recv()
    for c in range(4):
        s_acc1[c] = sb[b * 4 + c] + s_rx1[c]
    for r in range(1, 4):
        send(3, r, s_acc1.at[g ^ r], s_rx2.at[r], cross[r])
    for r in range(1, 4):
        reduced(2, r, e_acc1.at[g ^ r], e_rx2.at[r], cross[r]).wait_recv()
    e_acc2[...] = (
        e_acc1[g].astype(F32) + e_rx2[1].astype(F32) + e_rx2[2].astype(F32) + e_rx2[3].astype(F32)
    ).astype(BF)
    rows_of = lambda i: pl.ds(pl.multiple_of(i * piece, piece), piece)
    for r in range(1, z_count):
        send(4, r, e_acc2.at[rows_of(z ^ r)], e_rx3.at[r], along[r])
    for r in range(1, 4):
        reduced(3, r, s_acc1.at[g ^ r], s_rx2.at[r], cross[r]).wait_recv()
    s_rx3[z] = s_acc1[g] + s_rx2[1] + s_rx2[2] + s_rx2[3]
    for r in range(1, z_count):
        send(5, r, s_rx3.at[z], s_rx3.at[z], along[r])
    total = e_acc2[rows_of(z), :].astype(F32)
    for r in range(1, z_count):
        reduced(4, r, e_acc2.at[rows_of(z ^ r)], e_rx3.at[r], along[r]).wait_recv()
        total = total + e_rx3[r].astype(F32)
    e_piece[...] = total.astype(BF)
    own = b * 4 + g
    cols_of = lambda i: pl.ds(pl.multiple_of(i * lanes, lanes), lanes)
    for r in range(1, z_count):
        send(6, r, e_piece, big_ref.at[rows_of(z), cols_of(own)], along[r])
    big_ref[rows_of(z), cols_of(own)] = total.astype(BF)
    for r in range(1, z_count):
        reduced(5, r, s_rx3.at[z], s_rx3.at[z ^ r], along[r]).wait_recv()
    s_total = s_rx3[0]
    for i in range(1, z_count):
        s_total = s_total + s_rx3[i]
    small_ref[own] = s_total
    for r in range(1, 4):
        send(7, r, small_ref.at[own], small_ref.at[own], cross[r])
    for r in range(1, z_count):
        reduced(6, r, e_piece, big_ref.at[rows_of(z ^ r), cols_of(own)], along[r]).wait_recv()
    for r in range(1, 4):
        send(8, r, big_ref.at[:, cols_of(own)], big_ref.at[:, cols_of(own)], cross[r])
    for r in range(1, 4):
        reduced(7, r, small_ref.at[own], small_ref.at[b * 4 + (g ^ r)], cross[r]).wait_recv()
    send(9, 0, small_ref.at[mine], small_ref.at[mine], near)
    send(10, 0, big_ref.at[:, cols_of(own)], big_ref.at[:, cols_of(own)], near)
    for r in range(1, 4):
        theirs = b * 4 + (g ^ r)
        reduced(8, r, big_ref.at[:, cols_of(own)], big_ref.at[:, cols_of(theirs)], cross[r]).wait_recv()
        send(10, r, big_ref.at[:, cols_of(theirs)], big_ref.at[:, cols_of(theirs)], near)
    reduced(9, 0, small_ref.at[mine], small_ref.at[other], near).wait_recv()
    for r in range(4):
        theirs = (1 - b) * 4 + (g ^ r)
        reduced(10, r, big_ref.at[:, cols_of(theirs)], big_ref.at[:, cols_of(theirs)], near).wait_recv()
    for copy in sent:
        copy.wait_send()
    for copy in strips:
        copy.wait_send()

    @pl.loop(0, count)
    def _(k):
        @pl.when(k > 0)
        def _():
            rows_moves[0](k).wait_send()
            cots_moves[0](k).wait_send()
            back(k).wait_send()

        for copy in rows_moves[1:] + cots_moves[1:] + (sum_near_a, sum_near_b, sum_far):
            copy(k).wait_send()

    for end in ends:
        end()


def local(
    raw_tiles, stem_weight, embed_weight, norm_gain, router_weight, w_gate, w_up, w_down, routes,
    cotangent,
):
    tokens, width = cotangent.shape
    owners, members = lax.axis_size("de"), lax.axis_size("tp")
    experts = w_gate.shape[0] * owners
    cap = 2 * tokens // experts
    share = w_gate.shape[2]
    channels = raw_tiles.shape[0]
    stem = stem_weight.shape[0]
    patch_dim = embed_weight.shape[0]
    total = owners * members * cap
    shape = jax.ShapeDtypeStruct
    table = jnp.asarray(tap_table(channels), BF)
    taps = jnp.pad(stem_weight.reshape(stem, channels * 9), ((0, 0), (0, TAPS - channels * 9)))
    anywhere = pl.BlockSpec(memory_space=pl.ANY)
    lanes = width // 8
    z_count = owners // 2
    small_rows = experts + 16
    piece = patch_dim // z_count
    vmem, dma = pltpu.VMEM, pltpu.SemaphoreType.DMA
    mix, big, small, grad_gate, grad_up, grad_down = pl.pallas_call(
        step_kernel,
        out_shape=(
            shape((tokens, width), BF),
            shape((patch_dim, width), BF),
            shape((8, small_rows, lanes), F32),
            shape(w_gate.shape, F32),
            shape(w_up.shape, F32),
            shape(w_down.shape, F32),
        ),
        in_specs=[VMEM] * 6 + [anywhere] * 5,
        out_specs=(VMEM,) * 3 + (anywhere,) * 3,
        scratch_shapes=[
            vmem(table.shape, BF),
            vmem(embed_weight.shape, BF),
            vmem((width, share), BF),
            vmem((width, share), BF),
            vmem((share, width), BF),
            vmem((2,) + raw_tiles.shape, BF),
            vmem((experts, cap, width + 128), BF),
            vmem((experts, cap, width), BF),
            vmem((owners, members, cap, width + 128), BF),
            vmem((owners, members, cap, width), BF),
            vmem((owners, members, 2 * cap, width), BF),
            vmem((owners, 2, 2 * cap, width), BF),
            vmem((owners, 2 * cap, width), BF),
            vmem((owners, 2 * cap, width), BF),
            vmem((total, width), BF),
            vmem((total, width), BF),
            vmem((total, share), BF),
            vmem((total, share), BF),
            vmem((total, share), BF),
            vmem((3, width // 256, 256, width), F32),
            vmem((tokens, patch_dim), F32),
            vmem((tokens, patch_dim), BF),
            vmem((tokens, width), F32),
            vmem((tokens, 1), F32),
            vmem((tokens, width), BF),
            vmem((tokens, 1), F32),
            vmem((tokens, 1), jnp.int32),
            vmem((tokens, CLASSES * TAPS), BF),
            vmem((8, patch_dim, lanes), BF),
            vmem((4, patch_dim, lanes), BF),
            vmem((4, patch_dim, lanes), BF),
            vmem((4, patch_dim, lanes), BF),
            vmem((patch_dim, lanes), BF),
            vmem((z_count, piece, lanes), BF),
            vmem((piece, lanes), BF),
            vmem((8, small_rows, lanes), F32),
            vmem((4, small_rows, lanes), F32),
            vmem((4, small_rows, lanes), F32),
            vmem((4, small_rows, lanes), F32),
            vmem((z_count, small_rows, lanes), F32),
            dma((5,)),
            dma,
            dma((3, width // 256)),
            dma((2,)),
            dma((2,)),
            dma((12, owners)),
            dma((12, owners)),
            dma((11, max(4, z_count))),
            dma((11, max(4, z_count))),
        ],
        compiler_params=pltpu.CompilerParams(
            vmem_limit_bytes=58 << 20, collective_id=1, has_side_effects=True
        ),
        name="step",
    )(
        raw_tiles, taps, norm_gain.reshape(1, width), router_weight, routes, cotangent,
        table, embed_weight, w_gate, w_up, w_down,
    )
    grad_router = small[:, :experts].transpose(0, 2, 1).reshape(width, experts)
    grad_gain = small[:, experts].reshape(width)
    taps_grad = small[: stem // 8, experts + 8 :].reshape(stem, lanes)[:, : channels * 9]
    return (
        mix, grad_gate, grad_up, grad_down, grad_router, grad_gain, big.astype(F32),
        taps_grad.reshape(stem_weight.shape),
    )


def solution(mesh):
    tiles = P(("de", "tp"), None)
    columns, rows = P("de", None, "tp"), P("de", "tp", None)
    return jax.shard_map(
        local,
        mesh=mesh,
        in_specs=(
            P(None, ("de", "tp"), None), P(), P(), P(), P(), columns, columns, rows, tiles, tiles,
        ),
        out_specs=(tiles, columns, columns, rows, P(), P(), P(), P()),
        check_vma=False,
    )
```

time: 165 us -> 150 us (0.909)
  local copies, waits for them, and re-layouts: 29.4 us -> 19 us
  starting transfers between devices: 4.32 us -> 0 us
    unnamed x25 -> x17, local copies, waits for them, and re-layouts: 20.1 us -> 14.5 us
    ppermute x2 -> x0, starting transfers between devices: 4.32 us -> none  [the longest x1 3.03 us: windows(): low = lax.ppermute(raw[:, -1:], axes, forward)]
    convert_element_type x1 -> x0, local copies, waits for them, and re-layouts: 3.54 us -> none  [local(): grad_embed = big.transpose(1, 0, 2).reshape(patch_dim, width).astype(F32)]
    concatenate x2 -> x0, other arithmetic: 2.58 us -> none  [the longest x1 1.82 us: windows(): jnp.concatenate([left, grid, right], axis=3).reshape(cols // PATCH, -1)]
    pallas_call x3 -> x1, Pallas kernels: 125 us -> 126 us  [local(): pl.pallas_call(step_kernel, out_shape=(shape((tokens, width), BF), shape(...]
  transfers between devices with their start and end apart: 2 -> 0, of which waited for: 0 -> 0; matrix products, arithmetic and copies ran while one was open for 1% -> 0% of each run, Pallas kernels for 0% -> 0%
where the time goes in v2:
time: 150 us; the launch traced here: 149 us
  Pallas kernels  126 us (84%)
  local copies, waits for them, and re-layouts  19 us (13%)
  other arithmetic  3.46 us (2%)
    pallas_call x1, Pallas kernels, local(): pl.pallas_call(step_kernel, out_shape=(shape((tokens, width), BF), shape(...  126 us
    unnamed x17, local copies, waits for them, and re-layouts  14.5 us
    convert_element_type x1, other arithmetic, local(): big.astype(F32)  3.46 us

profile of v2, /device:TPU:0, one launch (start us, length us, event | category | flops | bytes accessed | tf_op | source)
XLA Modules:
  0.0 149.5 jit_solution(10417011414450497868)
XLA Ops:
  0.6 1.6 %copy.24.router_ref = bf16[1024,8]{1,0:T(8,128)(2,1)} copy(bf16[1024,8]{0,1:T(8,128)(2,1)} %param.15) | data formatting | bytes 32768 | tf_op args[4]
  2.2 1.4 copy.25.routes_ref
  3.6 0.7 copy.22
  4.3 0.1 copy.23
  4.4 0.6 pad.4.taps_ref
  5.0 126.3 %step.1 = (bf16[128,1024]{1,0:T(8,128)(2,1)}, bf16[768,1024]{1,0:T(8,128)(2,1)}, f32[8,24,128]{2,1,0:T(8,128)}, f32[1,1024,1024]{2,1,0:T(8,128)}, f32[1,1024,1024]{2,1,0:T(8,128)}, /*index=5*/f32[1,1024,1024]{2,1,0:T(8,128)}) custom-call(bf16[4,4,512]{2,1,0:T(4,128)(2,1)} %raw_ref.1, bf16[48,40]{1,0:T(8,128)(2,1)} %pad.4.taps_ref, f32[1,1024]{1,0:T(1,128)} %bitcast.14, ...), custom_call_target="tpu_custom_call" | custom-call | tf_op jit(solution)/shard_map/step/pallas_call | solution.py:534
  131.3 0.0 copy-start.3
  131.3 0.8 slice_bitcast_fusion.1
  132.1 0.1 copy.28
  132.2 0.0 copy-start.2
  132.2 0.6 copy.27
  132.8 1.7 %slice_bitcast_fusion = f32[1024,8]{0,1:T(8,128)} fusion(f32[8,24,128]{2,1,0:T(8,128)} %get-tuple-element.18), kind=kLoop, calls=%fused_computation | loop fusion | bytes 65536 | tf_op jit(solution)/shard_map/reshape | solution.py:605
  134.5 1.4 slice.13
  135.9 3.5 %convert_element_type.5 = f32[768,1024]{1,0:T(8,128)} convert(bf16[768,1024]{1,0:T(8,128)(2,1)} %get-tuple-element.19) | non-fusion elementwise | flops 786432 | bytes 4718592 | tf_op jit(solution)/shard_map/convert_element_type | solution.py:609
  139.3 0.0 copy-done.3
  139.3 0.7 copy.33
  140.0 0.0 copy-done.2
  140.0 0.0 copy-start.1
  140.0 2.1 %copy.34 = f32[1,1024,1024]{2,1,0:T(8,128)} copy(f32[1,1024,1024]{2,1,0:T(8,128)S(1)} %copy-done.2) | data formatting | bytes 8388608
  142.2 1.6 %copy-done.1 = f32[1,1024,1024]{2,1,0:T(8,128)S(1)} copy-done((f32[1,1024,1024]{2,1,0:T(8,128)S(1)}, f32[1,1024,1024]{2,1,0:T(8,128)}, u32[]{:S(2)}) %copy-start.1) | copy-done | bytes 4194328
  143.7 0.0 copy-start
  143.7 2.1 %copy.35 = f32[1,1024,1024]{2,1,0:T(8,128)} copy(f32[1,1024,1024]{2,1,0:T(8,128)S(1)} %copy-done.1) | data formatting | bytes 8388608
  145.9 1.6 %copy-done = f32[1,1024,1024]{2,1,0:T(8,128)S(1)} copy-done((f32[1,1024,1024]{2,1,0:T(8,128)S(1)}, f32[1,1024,1024]{2,1,0:T(8,128)}, u32[]{:S(2)}) %copy-start) | copy-done | bytes 4194328
  147.4 2.0 %copy.36 = f32[1,1024,1024]{2,1,0:T(8,128)} copy(f32[1,1024,1024]{2,1,0:T(8,128)S(1)} %copy-done) | data formatting | bytes 8388608
  (2 shorter events, 0.0 us)
Async XLA Ops:
  131.3 8.0 %copy-start.3 = (bf16[128,1024]{1,0:T(8,128)(2,1)S(1)}, bf16[128,1024]{1,0:T(8,128)(2,1)}, u32[]{:S(2)}) copy-start(bf16[128,1024]{1,0:T(8,128)(2,1)} %get-tuple-element.36) | copy-start | bytes 786436
  132.2 7.8 %copy-start.2 = (f32[1,1024,1024]{2,1,0:T(8,128)S(1)}, f32[1,1024,1024]{2,1,0:T(8,128)}, u32[]{:S(2)}) copy-start(f32[1,1024,1024]{2,1,0:T(8,128)} %get-tuple-element.37) | copy-start | bytes 12582916
  140.0 3.7 %copy-start.1 = (f32[1,1024,1024]{2,1,0:T(8,128)S(1)}, f32[1,1024,1024]{2,1,0:T(8,128)}, u32[]{:S(2)}) copy-start(f32[1,1024,1024]{2,1,0:T(8,128)} %get-tuple-element.38) | copy-start | bytes 12582916
  143.7 3.7 %copy-start = (f32[1,1024,1024]{2,1,0:T(8,128)S(1)}, f32[1,1024,1024]{2,1,0:T(8,128)}, u32[]{:S(2)}) copy-start(f32[1,1024,1024]{2,1,0:T(8,128)} %get-tuple-element.39) | copy-start | bytes 12582916

commit v3 on v2

--- a/solution.py
+++ b/solution.py
@@ -52,12 +52,12 @@
 def step_kernel(
     raw_ref, taps_ref, gain_ref, router_ref, routes_ref, cot_ref,
     table_hbm, embed_hbm, gate_ref, up_ref, down_ref,
-    mix_ref, big_ref, small_ref, ggate_ref, gup_ref, gdown_ref,
+    mix_ref, embed_out, router_out, gain_out, stem_out, ggate_ref, gup_ref, gdown_ref,
     table_ref, embed_ref, wg, wu, wd, halo, sent_r, sent_c, grp_r, grp_c, part, rx1, rx2, ret_ref,
     rows_all, cots_all, act_all, gcot_all, ucot_all, stage,
     preact_ref, patches_ref, embedded_ref, inv_ref, hidden_ref, score_ref, slot_ref, winall_ref,
     eb, e_rx1, e_acc1, e_rx2, e_acc2, e_rx3, e_piece, sb, s_rx1, s_acc1, s_rx2, s_rx3,
-    load_sem, own_sem, store_sem, halo_send, halo_recv, send_sem, recv_sem, red_send, red_recv,
+    big_ref, small_ref, load_sem, own_sem, store_sem, halo_send, halo_recv, send_sem, recv_sem, red_send, red_recv,
 ):
     count, members, cap, width = grp_c.shape
     tokens = cot_ref.shape[0]
@@ -88,6 +88,9 @@
     for load in loads:
         load.start()
 
+    def partner(k):
+        return me_e ^ (k // 2 + k % 2 * (count // 2))
+
     def remote(kind, k, src, dst, device):
         return pltpu.make_async_remote_copy(
             src_ref=src, dst_ref=dst, send_sem=send_sem.at[kind, k], recv_sem=recv_sem.at[kind, k],
@@ -96,7 +99,7 @@
 
     def moves(base, sent_ref, grp):
         return (
-            lambda k: remote(base, k, sent_ref.at[me_e ^ k], grp.at[k, 0], (me_e ^ k, me_t)),
+            lambda k: remote(base, k, sent_ref.at[partner(k)], grp.at[k, 0], (partner(k), me_t)),
             lambda k: remote(base + 1, k, grp.at[k, 0], grp.at[k, 1], near),
             lambda k: remote(base + 2, k, grp.at[k, 0], grp.at[k, 2], far),
             lambda k: remote(base + 3, k, grp.at[k, 2], grp.at[k, 3], near),
@@ -107,8 +110,8 @@
     sum_near_a = lambda k: remote(8, k, part.at[k, 1], rx1.at[k, 0], near)
     sum_near_b = lambda k: remote(9, k, part.at[k, 3], rx1.at[k, 1], near)
     sum_far = lambda k: remote(10, k, part.at[k, 2], rx2.at[k], far)
-    back = lambda k: remote(11, k, part.at[k, 0], ret_ref.at[me_e], (me_e ^ k, me_t))
-    back_in = lambda k: remote(11, k, part.at[k, 0], ret_ref.at[me_e ^ k], (me_e ^ k, me_t))
+    back = lambda k: remote(11, k, part.at[k, 0], ret_ref.at[me_e], (partner(k), me_t))
+    back_in = lambda k: remote(11, k, part.at[k, 0], ret_ref.at[partner(k)], (partner(k), me_t))
 
     place = me_e * members + me_t
     last = count * members - 1
@@ -143,9 +146,9 @@
             slot_ref[...] == lax.broadcasted_iota(jnp.int32, (tokens, experts * cap), 1)
         ).astype(BF)
 
-    def scatter(values, sent_ref, grp, move):
+    def scatter(values, sent_ref, grp, move, window_of):
         sent_ref[...] = mm(selector(), values, TN).reshape(sent_ref.shape).astype(BF)
-        for k in range(1, count):
+        for k in range(1, window_of):
             move[0](k).start()
         own = pltpu.make_async_copy(sent_ref.at[me_e], grp.at[0, 0], own_sem)
         own.start()
@@ -153,7 +156,7 @@
         move[2](0).start()
         move[1](0).start()
 
-    scatter(cot_ref[...], sent_c, grp_c, cots_moves)
+    scatter(cot_ref[...], sent_c, grp_c, cots_moves, count)
 
     for strip_copy in strips:
         strip_copy.wait_recv()
@@ -207,7 +210,7 @@
     tail = jnp.where(
         lane == 0, first, jnp.where(lane == 1, second, jnp.where(lane == 2, third, 0.0))
     )
-    scatter(jnp.concatenate([hidden, tail.astype(BF)], axis=1), sent_r, grp_r, rows_moves)
+    scatter(jnp.concatenate([hidden, tail.astype(BF)], axis=1), sent_r, grp_r, rows_moves, 2)
 
     def forward(k, move):
         @pl.when(k > 0)
@@ -297,6 +300,10 @@
     def _(k):
         forward(k, cots_moves)
 
+        @pl.when(k < count - 1)
+        def _():
+            rows_moves[0](k + 1).start()
+
     forward_rows(0)
     for load in loads[2:]:
         load.wait()
@@ -313,6 +320,11 @@
         settle(p, cots_moves)
         settle(p, rows_moves)
         gather(p)
+
+        @pl.when(p >= 1)
+        def _():
+            reduce_near(p - 1)
+
         compute(p)
         for i in range(per):
             k = p * per + i
@@ -321,11 +333,7 @@
 
         @pl.when(p >= 1)
         def _():
-            reduce_near(p - 1)
-
-        @pl.when(p >= 2)
-        def _():
-            reduce_far(p - 2)
+            reduce_far(p - 1)
 
     half = 256
 
@@ -334,25 +342,27 @@
 
         def store(c):
             return pltpu.make_async_copy(
-                stage.at[j, c], out_ref.at[0, pl.ds(pl.multiple_of(c * half, half), half), :],
-                store_sem.at[j, c],
+                stage.at[j, c % 2], out_ref.at[0, pl.ds(pl.multiple_of(c * half, half), half), :],
+                store_sem.at[j, c % 2],
             )
 
         @pl.loop(0, n)
         def _(c):
+            @pl.when(c >= 2)
+            def _():
+                store(c - 2).wait()
+
             at = pl.ds(pl.multiple_of(c * half, half), half)
-            stage[j, c] = mm(lhs[:, at], rhs[...], TN)
+            stage[j, c % 2] = mm(lhs[:, at], rhs[...], TN)
             store(c).start()
 
         def finish():
-            for c in range(n):
+            for c in range(max(0, n - 2), n):
                 store(c).wait()
 
         return finish
 
     reduce_near(steps - 1)
-    if steps >= 2:
-        reduce_far(steps - 2)
     ends = [grads(0, rows_all, gcot_all, ggate_ref)]
     reduce_far(steps - 1)
     own_back = pltpu.make_async_copy(part.at[0, 0], ret_ref.at[me_e], own_sem)
@@ -485,10 +495,23 @@
         theirs = b * 4 + (g ^ r)
         reduced(8, r, big_ref.at[:, cols_of(own)], big_ref.at[:, cols_of(theirs)], cross[r]).wait_recv()
         send(10, r, big_ref.at[:, cols_of(theirs)], big_ref.at[:, cols_of(theirs)], near)
+
+    def widen(i):
+        embed_out[:, cols_of(i)] = big_ref[:, cols_of(i)].astype(F32)
+
+    for r in range(4):
+        widen(b * 4 + (g ^ r))
     reduced(9, 0, small_ref.at[mine], small_ref.at[other], near).wait_recv()
     for r in range(4):
         theirs = (1 - b) * 4 + (g ^ r)
         reduced(10, r, big_ref.at[:, cols_of(theirs)], big_ref.at[:, cols_of(theirs)], near).wait_recv()
+        widen(theirs)
+    for c in range(chunks):
+        at = slice(c * lanes, (c + 1) * lanes)
+        router_out[:, at] = small_ref[c, :experts]
+        gain_out[:, at] = small_ref[c, experts : experts + 1]
+        if c * 8 < stem:
+            stem_out[c * 8 : c * 8 + 8] = small_ref[c, experts + 8 :]
     for copy in sent:
         copy.wait_send()
     for copy in strips:
@@ -531,18 +554,20 @@
     small_rows = experts + 16
     piece = patch_dim // z_count
     vmem, dma = pltpu.VMEM, pltpu.SemaphoreType.DMA
-    mix, big, small, grad_gate, grad_up, grad_down = pl.pallas_call(
+    mix, grad_embed, router_rows, grad_gain, taps_grad, grad_gate, grad_up, grad_down = pl.pallas_call(
         step_kernel,
         out_shape=(
             shape((tokens, width), BF),
-            shape((patch_dim, width), BF),
-            shape((8, small_rows, lanes), F32),
+            shape((patch_dim, width), F32),
+            shape((experts, width), F32),
+            shape((1, width), F32),
+            shape((stem, lanes), F32),
             shape(w_gate.shape, F32),
             shape(w_up.shape, F32),
             shape(w_down.shape, F32),
         ),
         in_specs=[VMEM] * 6 + [anywhere] * 5,
-        out_specs=(VMEM,) * 3 + (anywhere,) * 3,
+        out_specs=(VMEM,) * 5 + (anywhere,) * 3,
         scratch_shapes=[
             vmem(table.shape, BF),
             vmem(embed_weight.shape, BF),
@@ -563,7 +588,7 @@
             vmem((total, share), BF),
             vmem((total, share), BF),
             vmem((total, share), BF),
-            vmem((3, width // 256, 256, width), F32),
+            vmem((3, 2, 256, width), F32),
             vmem((tokens, patch_dim), F32),
             vmem((tokens, patch_dim), BF),
             vmem((tokens, width), F32),
@@ -584,9 +609,11 @@
             vmem((4, small_rows, lanes), F32),
             vmem((4, small_rows, lanes), F32),
             vmem((z_count, small_rows, lanes), F32),
+            vmem((patch_dim, width), BF),
+            vmem((8, small_rows, lanes), F32),
             dma((5,)),
             dma,
-            dma((3, width // 256)),
+            dma((3, 2)),
             dma((2,)),
             dma((2,)),
             dma((12, owners)),
@@ -595,19 +622,16 @@
             dma((11, max(4, z_count))),
         ],
         compiler_params=pltpu.CompilerParams(
-            vmem_limit_bytes=58 << 20, collective_id=1, has_side_effects=True
+            vmem_limit_bytes=52 << 20, collective_id=1, has_side_effects=True
         ),
         name="step",
     )(
         raw_tiles, taps, norm_gain.reshape(1, width), router_weight, routes, cotangent,
         table, embed_weight, w_gate, w_up, w_down,
     )
-    grad_router = small[:, :experts].transpose(0, 2, 1).reshape(width, experts)
-    grad_gain = small[:, experts].reshape(width)
-    taps_grad = small[: stem // 8, experts + 8 :].reshape(stem, lanes)[:, : channels * 9]
     return (
-        mix, grad_gate, grad_up, grad_down, grad_router, grad_gain, big.astype(F32),
-        taps_grad.reshape(stem_weight.shape),
+        mix, grad_gate, grad_up, grad_down, router_rows.T, grad_gain.reshape(width), grad_embed,
+        taps_grad[:, : channels * 9].reshape(stem_weight.shape),
     )
 
 

time: 150 us -> 148 us (0.987)
  other arithmetic: 3.46 us -> 0 us
  local copies, waits for them, and re-layouts: 19 us -> 20.9 us
    unnamed x17 -> x25, local copies, waits for them, and re-layouts: 14.5 us -> 20.7 us
    convert_element_type x1 -> x0, other arithmetic: 3.46 us -> none  [local(): big.astype(F32)]
    reshape x3 -> x1, local copies, waits for them, and re-layouts: 2.49 us -> 0.01 us  [local(): taps_grad[:, :channels * 9].reshape(stem_weight.shape)]
where the time goes in v3:
time: 148 us; the launch traced here: 147 us
  Pallas kernels  125 us (84%)
  local copies, waits for them, and re-layouts  20.9 us (14%)
    pallas_call x1, Pallas kernels, local(): pl.pallas_call(step_kernel, out_shape=(shape((tokens, width), BF), shape(...  125 us
    unnamed x25, local copies, waits for them, and re-layouts  20.7 us

profile of v3, /device:TPU:0, one launch (start us, length us, event | category | flops | bytes accessed | tf_op | source)
XLA Modules:
  0.0 147.1 jit_solution(7331026609596141618)
XLA Ops:
  0.6 0.7 copy.23
  1.4 0.1 copy.24
  1.5 0.8 copy.26.routes_ref
  2.2 0.9 copy.25.router_ref
  3.1 0.0 copy-start
  3.1 0.9 copy-done
  4.1 0.0 copy-start.1
  4.1 0.9 copy-done.1
  5.0 0.0 copy-start.2
  5.0 0.7 copy-done.2
  5.7 0.0 copy-start.3
  5.8 0.7 copy-done.3
  6.4 125.5 %step.1 = (bf16[128,1024]{1,0:T(8,128)(2,1)S(1)}, f32[768,1024]{1,0:T(8,128)}, f32[8,1024]{1,0:T(8,128)S(1)}, f32[1,1024]{1,0:T(1,128)S(1)}, f32[48,128]{1,0:T(8...) custom-call(bf16[4,4,512]{2,1,0:T(4,128)(2,1)S(1)} %copy-done.2, ...), custom_call_target="tpu_custom_call" | custom-call | tf_op jit(solution)/shard_map/step/pallas_call | solution.py:557
  131.9 0.1 copy.27
  132.0 0.6 copy.28
  132.6 0.7 copy.36
  133.3 0.0 copy-start.5
  133.3 4.9 %copy.37 = f32[1,1024,1024]{2,1,0:T(8,128)} copy(f32[1,1024,1024]{2,1,0:T(8,128)} %get-tuple-element.49) | data formatting | bytes 8388608
  138.3 0.0 copy-done.5
  138.3 0.0 copy-start.4
  138.3 2.1 %copy.38 = f32[1,1024,1024]{2,1,0:T(8,128)} copy(f32[1,1024,1024]{2,1,0:T(8,128)S(1)} %copy-done.5) | data formatting | bytes 8388608
  140.4 1.6 %copy-done.4 = f32[1,1024,1024]{2,1,0:T(8,128)S(1)} copy-done((f32[1,1024,1024]{2,1,0:T(8,128)S(1)}, f32[1,1024,1024]{2,1,0:T(8,128)}, u32[]{:S(2)}) %copy-start.4) | copy-done | bytes 4194328
  142.0 0.0 copy-start.6
  142.0 2.1 %copy.39 = f32[1,1024,1024]{2,1,0:T(8,128)} copy(f32[1,1024,1024]{2,1,0:T(8,128)S(1)} %copy-done.4) | data formatting | bytes 8388608
  144.1 0.6 copy.40
  144.7 0.6 copy.41
  145.3 0.1 copy-done.6
  145.4 1.7 %copy.42 = f32[768,1024]{1,0:T(8,128)} copy(f32[768,1024]{1,0:T(8,128)S(1)} %copy-done.6) | data formatting | bytes 6291456
  (3 shorter events, 0.0 us)
Async XLA Ops:
  3.1 1.0 copy-start
  4.1 0.9 copy-start.1
  5.0 0.7 copy-start.2
  5.7 0.7 copy-start.3
  133.3 4.9 %copy-start.5 = (f32[1,1024,1024]{2,1,0:T(8,128)S(1)}, f32[1,1024,1024]{2,1,0:T(8,128)}, u32[]{:S(2)}) copy-start(f32[1,1024,1024]{2,1,0:T(8,128)} %get-tuple-element.50) | copy-start | bytes 12582916
  138.3 3.7 %copy-start.4 = (f32[1,1024,1024]{2,1,0:T(8,128)S(1)}, f32[1,1024,1024]{2,1,0:T(8,128)}, u32[]{:S(2)}) copy-start(f32[1,1024,1024]{2,1,0:T(8,128)} %get-tuple-element.51) | copy-start | bytes 12582916
  142.0 3.4 %copy-start.6 = (f32[768,1024]{1,0:T(8,128)S(1)}, f32[768,1024]{1,0:T(8,128)}, u32[]{:S(2)}) copy-start(f32[768,1024]{1,0:T(8,128)} %get-tuple-element.54) | copy-start | bytes 9437188

commit v4 on v3

--- a/solution.py
+++ b/solution.py
@@ -11,6 +11,7 @@
 GELU_A = 0.044715
 EPSILON = 1e-06
 TAPS = 40
+BATCH = 512
 CLASSES = PATCH * PATCH
 MESH = pl.DeviceIdType.MESH
 BF = jnp.bfloat16
@@ -53,7 +54,7 @@
     raw_ref, taps_ref, gain_ref, router_ref, routes_ref, cot_ref,
     table_hbm, embed_hbm, gate_ref, up_ref, down_ref,
     mix_ref, embed_out, router_out, gain_out, stem_out, ggate_ref, gup_ref, gdown_ref,
-    table_ref, embed_ref, wg, wu, wd, halo, sent_r, sent_c, grp_r, grp_c, part, rx1, rx2, ret_ref,
+    table_ref, embed_ref, wg, wu, wd, wg_t, wu_t, wd_t, halo, sent_r, sent_c, grp_r, grp_c, part, rx1, rx2, ret_ref,
     rows_all, cots_all, act_all, gcot_all, ucot_all, stage,
     preact_ref, patches_ref, embedded_ref, inv_ref, hidden_ref, score_ref, slot_ref, winall_ref,
     eb, e_rx1, e_acc1, e_rx2, e_acc2, e_rx3, e_piece, sb, s_rx1, s_acc1, s_rx2, s_rx3,
@@ -66,7 +67,7 @@
     stem = taps_ref.shape[0]
     channels, strip, pixel_cols = raw_ref.shape
     me_e, me_t = lax.axis_index("de"), lax.axis_index("tp")
-    batch = 256
+    batch = BATCH
     per = batch // (members * cap)
     steps = count // per
     chunks, patch_dim, lanes = eb.shape
@@ -250,7 +251,7 @@
 
     tile = 256
 
-    def compute(p):
+    def hidden_units(p):
         at = pl.ds(pl.multiple_of(p * batch, batch), batch)
 
         @pl.loop(0, share // tile)
@@ -258,18 +259,21 @@
             cols = pl.ds(pl.multiple_of(f * tile, tile), tile)
             gate = mm(rows_all[at, :], wg[:, cols])
             up = mm(rows_all[at, :], wu[:, cols])
-            act_cot = mm(cots_all[at, :], wd[cols, :], NT)
+            act_cot = mm(cots_all[at, :], wd_t[:, cols])
             sig = jax.nn.sigmoid(gate)
             activated = gate * sig
             act_all[at, cols] = (activated * up).astype(BF)
             gcot_all[at, cols] = (act_cot * up * (sig * (1.0 + gate * (1.0 - sig)))).astype(BF)
             ucot_all[at, cols] = (act_cot * activated).astype(BF)
 
+    def results(p):
+        at = pl.ds(pl.multiple_of(p * batch, batch), batch)
+
         @pl.loop(0, width // tile)
         def _(x):
             cols = pl.ds(pl.multiple_of(x * tile, tile), tile)
             out = mm(act_all[at, :], wd[:, cols])
-            back_cot = mm(gcot_all[at, :], wg[cols, :], NT) + mm(ucot_all[at, :], wu[cols, :], NT)
+            back_cot = mm(gcot_all[at, :], wg_t[:, cols]) + mm(ucot_all[at, :], wu_t[:, cols])
             both = jnp.concatenate(
                 [out.reshape(per, members, cap, tile), back_cot.reshape(per, members, cap, tile)],
                 axis=2,
@@ -296,6 +300,15 @@
             def _():
                 back(k).start()
 
+    for load in loads[2:]:
+        load.wait()
+    pieces = width // 128
+
+    def turn(i):
+        at = pl.ds(pl.multiple_of(i * 128, 128), 128)
+        for plain, turned in ((wg, wg_t), (wu, wu_t), (wd, wd_t)):
+            turned[:, at] = plain[at, :].T
+
     @pl.loop(1, count)
     def _(k):
         forward(k, cots_moves)
@@ -304,17 +317,17 @@
         def _():
             rows_moves[0](k + 1).start()
 
+        @pl.when(k <= pieces)
+        def _():
+            turn(k - 1)
+
+    for i in range(count - 1, pieces):
+        turn(i)
     forward_rows(0)
-    for load in loads[2:]:
-        load.wait()
 
     @pl.loop(0, steps)
     def _(p):
         arrive(p, cots_moves)
-
-        @pl.when(p < steps - 1)
-        def _():
-            forward_rows(p + 1)
 
         arrive(p, rows_moves)
         settle(p, cots_moves)
@@ -325,49 +338,52 @@
         def _():
             reduce_near(p - 1)
 
-        compute(p)
+        hidden_units(p)
+
+        @pl.when(p < steps - 1)
+        def _():
+            forward_rows(p + 1)
+
+        @pl.when(p >= 1)
+        def _():
+            reduce_far(p - 1)
+
+        results(p)
         for i in range(per):
             k = p * per + i
             sum_near_a(k).start()
             sum_near_b(k).start()
 
-        @pl.when(p >= 1)
-        def _():
-            reduce_far(p - 1)
-
-    half = 256
-
-    def grads(j, lhs, rhs, out_ref):
-        n = width // half
-
-        def store(c):
-            return pltpu.make_async_copy(
-                stage.at[j, c % 2], out_ref.at[0, pl.ds(pl.multiple_of(c * half, half), half), :],
-                store_sem.at[j, c % 2],
-            )
-
-        @pl.loop(0, n)
-        def _(c):
-            @pl.when(c >= 2)
-            def _():
-                store(c - 2).wait()
-
-            at = pl.ds(pl.multiple_of(c * half, half), half)
-            stage[j, c % 2] = mm(lhs[:, at], rhs[...], TN)
-            store(c).start()
-
-        def finish():
-            for c in range(max(0, n - 2), n):
-                store(c).wait()
-
-        return finish
-
+    half = 512
+
+    def grads(c, lhs, pairs):
+        turned = wd_t.at[pl.ds(0, half)]
+        turned[...] = lhs[:, c * half : (c + 1) * half].T
+        for j, rhs, out_ref in pairs:
+            for n in range(width // half):
+                at = pl.ds(n * half, half)
+
+                def store(row):
+                    return pltpu.make_async_copy(
+                        stage.at[j, n], out_ref.at[0, pl.ds(row * half, half), at], store_sem.at[j, n]
+                    )
+
+                if c:
+                    store(c - 1).wait()
+                stage[j, n] = mm(turned[...], rhs[:, at])
+                store(c).start()
+                if c == width // half - 1:
+                    ends.append(store(c))
+
+    ends = []
+    by_rows = [(0, gcot_all, ggate_ref), (1, ucot_all, gup_ref)]
+    by_act = [(2, cots_all, gdown_ref)]
     reduce_near(steps - 1)
-    ends = [grads(0, rows_all, gcot_all, ggate_ref)]
+    grads(0, rows_all, by_rows)
     reduce_far(steps - 1)
     own_back = pltpu.make_async_copy(part.at[0, 0], ret_ref.at[me_e], own_sem)
     own_back.start()
-    ends.append(grads(1, rows_all, ucot_all, gup_ref))
+    grads(1, rows_all, by_rows)
     own_back.wait()
     for k in range(1, count):
         back_in(k).wait_recv()
@@ -441,17 +457,18 @@
         )
     send(1, 0, sb.at[other], s_rx1, near)
 
+    grads(0, act_all, by_act)
     reduced(0, 0, eb.at[other], e_rx1, near).wait_recv()
     for c in range(4):
         e_acc1[c] = (eb[b * 4 + c].astype(F32) + e_rx1[c].astype(F32)).astype(BF)
     for r in range(1, 4):
         send(2, r, e_acc1.at[g ^ r], e_rx2.at[r], cross[r])
-    ends.append(grads(2, act_all, cots_all, gdown_ref))
     reduced(1, 0, sb.at[other], s_rx1, near).wait_recv()
     for c in range(4):
         s_acc1[c] = sb[b * 4 + c] + s_rx1[c]
     for r in range(1, 4):
         send(3, r, s_acc1.at[g ^ r], s_rx2.at[r], cross[r])
+    grads(1, act_all, by_act)
     for r in range(1, 4):
         reduced(2, r, e_acc1.at[g ^ r], e_rx2.at[r], cross[r]).wait_recv()
     e_acc2[...] = (
@@ -529,7 +546,7 @@
             copy(k).wait_send()
 
     for end in ends:
-        end()
+        end.wait()
 
 
 def local(
@@ -574,6 +591,9 @@
             vmem((width, share), BF),
             vmem((width, share), BF),
             vmem((share, width), BF),
+            vmem((share, width), BF),
+            vmem((share, width), BF),
+            vmem((width, share), BF),
             vmem((2,) + raw_tiles.shape, BF),
             vmem((experts, cap, width + 128), BF),
             vmem((experts, cap, width), BF),
@@ -588,7 +608,7 @@
             vmem((total, share), BF),
             vmem((total, share), BF),
             vmem((total, share), BF),
-            vmem((3, 2, 256, width), F32),
+            vmem((3, 2, 512, width // 2), F32),
             vmem((tokens, patch_dim), F32),
             vmem((tokens, patch_dim), BF),
             vmem((tokens, width), F32),
@@ -622,7 +642,7 @@
             dma((11, max(4, z_count))),
         ],
         compiler_params=pltpu.CompilerParams(
-            vmem_limit_bytes=52 << 20, collective_id=1, has_side_effects=True
+            vmem_limit_bytes=60 << 20, collective_id=1, has_side_effects=True
         ),
         name="step",
     )(

time: 148 us -> 151 us (1.020)
  Pallas kernels: 125 us -> 128 us
    pallas_call x1, Pallas kernels: 125 us -> 128 us  [local(): pl.pallas_call(step_kernel, out_shape=(shape((tokens, width), BF), shape(...]
    unnamed x25 -> x21, local copies, waits for them, and re-layouts: 20.7 us -> 19.7 us
where the time goes in v4:
time: 151 us; the launch traced here: 150 us
  Pallas kernels  128 us (85%)
  local copies, waits for them, and re-layouts  21.2 us (14%)
    pallas_call x1, Pallas kernels, local(): pl.pallas_call(step_kernel, out_shape=(shape((tokens, width), BF), shape(...  128 us
    unnamed x21, local copies, waits for them, and re-layouts  19.7 us

profile of v4, /device:TPU:0, one launch (start us, length us, event | category | flops | bytes accessed | tf_op | source)
XLA Modules:
  0.0 150.2 jit_solution(13438333628060518206)
XLA Ops:
  0.6 0.7 copy.23
  1.4 0.1 copy.24
  1.5 0.6 pad.4.taps_ref
  2.1 1.4 copy.26.routes_ref
  3.5 1.6 %copy.25.router_ref = bf16[1024,8]{1,0:T(8,128)(2,1)} copy(bf16[1024,8]{0,1:T(8,128)(2,1)} %param.15) | data formatting | bytes 32768 | tf_op args[4]
  5.0 128.3 %step.1 = (bf16[128,1024]{1,0:T(8,128)(2,1)}, f32[768,1024]{1,0:T(8,128)}, f32[8,1024]{1,0:T(8,128)}, f32[1,1024]{1,0:T(1,128)}, f32[48,128]{1,0:T(8,128)}, /*in...) custom-call(bf16[4,4,512]{2,1,0:T(4,128)(2,1)} %raw_ref.1, bf16[48,40]{1,0:T(8,128)(2,1)} %pad.4.taps_ref, ...), custom_call_target="tpu_custom_call" | custom-call | tf_op jit(solution)/shard_map/step/pallas_call | solution.py:574
  133.4 0.8 copy.27
  134.2 0.6 copy.28
  134.8 1.7 %copy.36 = bf16[128,1024]{1,0:T(8,128)(2,1)} copy(bf16[128,1024]{1,0:T(8,128)(2,1)} %get-tuple-element.48) | data formatting | bytes 524288
  136.5 0.0 copy-start.1
  136.5 4.9 %copy.37 = f32[1,1024,1024]{2,1,0:T(8,128)} copy(f32[1,1024,1024]{2,1,0:T(8,128)} %get-tuple-element.49) | data formatting | bytes 8388608
  141.4 0.0 copy-done.1
  141.4 0.0 copy-start
  141.4 2.1 %copy.38 = f32[1,1024,1024]{2,1,0:T(8,128)} copy(f32[1,1024,1024]{2,1,0:T(8,128)S(1)} %copy-done.1) | data formatting | bytes 8388608
  143.6 1.6 %copy-done = f32[1,1024,1024]{2,1,0:T(8,128)S(1)} copy-done((f32[1,1024,1024]{2,1,0:T(8,128)S(1)}, f32[1,1024,1024]{2,1,0:T(8,128)}, u32[]{:S(2)}) %copy-start) | copy-done | bytes 4194328
  145.1 0.0 copy-start.3
  145.1 0.0 copy-start.4
  145.1 0.0 copy-start.2
  145.1 2.1 %copy.39 = f32[1,1024,1024]{2,1,0:T(8,128)} copy(f32[1,1024,1024]{2,1,0:T(8,128)S(1)} %copy-done) | data formatting | bytes 8388608
  147.3 0.0 copy-done.3
  147.3 0.6 copy.40
  147.9 0.0 copy-done.4
  147.9 0.6 copy.41
  148.5 0.1 copy-done.2
  148.6 1.7 %copy.42 = f32[768,1024]{1,0:T(8,128)} copy(f32[768,1024]{1,0:T(8,128)S(1)} %copy-done.2) | data formatting | bytes 6291456
  (2 shorter events, 0.0 us)
Async XLA Ops:
  136.5 4.9 %copy-start.1 = (f32[1,1024,1024]{2,1,0:T(8,128)S(1)}, f32[1,1024,1024]{2,1,0:T(8,128)}, u32[]{:S(2)}) copy-start(f32[1,1024,1024]{2,1,0:T(8,128)} %get-tuple-element.50) | copy-start | bytes 12582916
  141.4 3.7 %copy-start = (f32[1,1024,1024]{2,1,0:T(8,128)S(1)}, f32[1,1024,1024]{2,1,0:T(8,128)}, u32[]{:S(2)}) copy-start(f32[1,1024,1024]{2,1,0:T(8,128)} %get-tuple-element.51) | copy-start | bytes 12582916
  145.1 2.1 %copy-start.3 = (f32[8,1024]{1,0:T(8,128)S(1)}, f32[8,1024]{1,0:T(8,128)}, u32[]{:S(2)}) copy-start(f32[8,1024]{1,0:T(8,128)} %get-tuple-element.20) | copy-start | bytes 98308
  145.1 2.8 %copy-start.4 = (f32[1,1024]{1,0:T(1,128)S(1)}, f32[1,1024]{1,0:T(1,128)}, u32[]{:S(2)}) copy-start(f32[1,1024]{1,0:T(1,128)} %get-tuple-element.21) | copy-start | bytes 12292
  145.1 3.4 %copy-start.2 = (f32[768,1024]{1,0:T(8,128)S(1)}, f32[768,1024]{1,0:T(8,128)}, u32[]{:S(2)}) copy-start(f32[768,1024]{1,0:T(8,128)} %get-tuple-element.54) | copy-start | bytes 9437188
